TPU v7x, 256 devices: a whole 4x4x8 slice. The times are simulated.
256 devices in a mesh: dp: 8 (over y_lo, x), expert: 32 (over z, y_hi, core).
Axes of the slice: x: 4, y: 4 (y_hi: 2, y_lo: 2; y = y_hi * 2 + y_lo), z: 8, core: 2. Of those that a mesh axis runs over, the one named last changes fastest.
Arguments:
- hidden: bfloat16 [12288, 8, 768], P('expert'), may hold values from -6 to 6
- expert_ids: int32 [12288, 8], P('expert'), may hold values from 0 to 63, all different within a row; in each aligned block of 384 rows (0 to 383, 384 to 767, ...) at most 96 rows name the same one
- route_gates: float32 [12288, 8], P('expert'), may hold values from 0.05 to 0.45
- down_weight: bfloat16 [64, 768, 2048], P('expert', None, 'dp'), may hold values from -0.21875 to 0.21875
Outputs:
- mixed: bfloat16 [12288, 2048], P('expert')
Inputs may be any that keep to these rules, and one draw needn't show every extreme that they name: `expert_ids`: each row names 8 different experts. Among the 384 tokens of one device (aligned blocks of 384 rows) no expert is named by more than 96 rows, and in at least one block some expert is named by exactly 96 rows.
All inputs are finite; a program needn't handle non-finite values.
Results may differ from a plain program's by a relative error of at most 0.0049.
Values may be sent and summed in bfloat16 or wider, within the bound.
A program may use at most 64 MiB of HBM per device.

v0:
```python
import math

import jax
import jax.numpy as jnp
from jax import lax
from jax.sharding import PartitionSpec as P


def passed_along(value, axis, steps):
    count = lax.axis_size(axis)
    pairs = [(source, (source + steps) % count) for source in range(count)]
    return lax.ppermute(value, axis, pairs)


def expert_products(picked, weights):
    return jnp.einsum("cef,efd->ced", picked, weights, preferred_element_type=jnp.float32).astype(
        jnp.bfloat16
    )


def route_positions(flat_ids, expert_total):
    route_total = flat_ids.shape[0]
    block_rows = math.gcd(route_total, 128)
    block_count = route_total // block_rows
    expert_range = jnp.arange(expert_total, dtype=jnp.int32)
    onehot = flat_ids[:, None] == expert_range[None, :]
    onehot_blocks = onehot.astype(jnp.bfloat16).reshape(block_count, block_rows, expert_total)
    row_range = jnp.arange(block_rows, dtype=jnp.int32)
    lower = (row_range[:, None] > row_range[None, :]).astype(jnp.bfloat16)
    within = jnp.einsum("ij,njk->nik", lower, onehot_blocks, preferred_element_type=jnp.float32)
    block_totals = jnp.sum(onehot_blocks.astype(jnp.float32), axis=1)
    offsets = jnp.cumsum(block_totals, axis=0) - block_totals
    earlier = (within + offsets[:, None, :]).reshape(route_total, expert_total)
    position = jnp.sum(jnp.where(onehot, earlier, 0.0), axis=1)
    return position.astype(jnp.int32)


def local(hidden, expert_ids, route_gates, down_weight):
    token_count, top_count, hidden_width = hidden.shape
    local_experts, _, columns = down_weight.shape
    loop_size = lax.axis_size("expert")
    expert_total = local_experts * loop_size
    capacity = token_count * top_count * 2 // expert_total
    route_total = token_count * top_count
    flat_ids = expert_ids.reshape(route_total)
    position = route_positions(flat_ids, expert_total)
    owner_of = flat_ids // local_experts
    local_of = flat_ids % local_experts
    slot_index = (owner_of * capacity + position) * local_experts + local_of
    route_range = jnp.arange(route_total, dtype=jnp.int32)
    slot_table = (
        jnp.full((expert_total * capacity,), route_total, jnp.int32).at[slot_index].set(route_range)
    )
    row_table = jnp.concatenate(
        [hidden.reshape(route_total, hidden_width), jnp.zeros((1, hidden_width), hidden.dtype)],
        axis=0,
    )
    outgoing = row_table[slot_table].reshape(loop_size, capacity, local_experts, hidden_width)
    device_here = lax.axis_index("expert")
    blank_results = jnp.zeros((loop_size, capacity, local_experts, columns), jnp.bfloat16)

    def apply_owner(results, weights, owner_index):
        picked = lax.dynamic_index_in_dim(outgoing, owner_index, 0, keepdims=False)
        product = expert_products(picked, weights)
        return lax.dynamic_update_index_in_dim(results, product, owner_index, 0)

    results = apply_owner(blank_results, down_weight, device_here)

    def one_hop(hop_index, loop_state):
        weights, results = loop_state
        weights = passed_along(weights, "expert", 1)
        owner_index = (device_here - hop_index) % loop_size
        return (weights, apply_owner(results, weights, owner_index))

    _, results = lax.fori_loop(1, loop_size, one_hop, (down_weight, results))
    per_route = results.reshape(expert_total * capacity, columns)[slot_index].astype(jnp.float32)
    weighted = per_route.reshape(token_count, top_count, columns) * route_gates[:, :, None]
    mixed_part = jnp.sum(weighted, axis=1).astype(jnp.bfloat16)
    return lax.all_gather(mixed_part, "dp", axis=1, tiled=True)


def solution(mesh):
    placed = (
        P("expert", None, None),
        P("expert", None),
        P("expert", None),
        P("expert", None, "dp"),
    )
    return jax.shard_map(
        local, mesh=mesh, in_specs=placed, out_specs=P("expert", None), check_vma=False
    )
```

profile of v0, /device:TPU:16, one launch (start us, length us, event | category | flops | bytes accessed | tf_op | source)
XLA Modules:
  0.0 696.6 jit_solution(4202359810127194261)
XLA Ops:
  26.4 31.0 %gather_fusion = bf16[6144,768]{1,0:T(8,128)(2,1)} fusion(bf16[3073,768]{1,0:T(8,128)(2,1)} %concatenate.3, s32[6144]{0:T(1024)S(1)} %fusion.17), kind=kCustom, calls=%fused_computation | custom fusion | bytes 18898944 | tf_op jit(solution)/shard_map/gather | solution.py:58
  57.4 19.2 %reshape.184 = bf16[32,96,2,768]{3,2,1,0:T(2,128)(2,1)} reshape(bf16[6144,768]{1,0:T(8,128)(2,1)} %gather_fusion) | data formatting | bytes 18874368 | tf_op jit(solution)/shard_map/reshape | solution.py:58
  89.2 510.1 %while.17 = (s32[]{:T(128)}, bf16[2,768,256]{2,1,0:T(8,128)(2,1)S(1)}, bf16[32,96,2,256]{3,1,2,0:T(8,128)(2,1)}, s32[]{:T(128)}, bf16[32,96,2,768]{3,1,2,0:T(8,1...) while((s32[]{:T(128)}, bf16[2,768,256]{2,1,0:T(8,128)(2,1)S(1)}, ...), condition=%wide.region_5.6_spmd, body=%wide.region_4.5_spmd.sunk | while | flops 75546640 | bytes 5899552 | solution.py:75
  89.2 12.9 %collective-permute-done = bf16[2,768,256]{2,1,0:T(8,128)(2,1)S(1)} collective-permute-done((bf16[2,768,256]{2,1,0:T(8,128)(2,1)S(1)}, bf16[2,768,256]{2,1,0:T(8,128)(2,1)S(1)}, u32[]{:S(2)}, u32[]{:S(2)}) %collective-permute-start) | collective-permute-done | bytes 786464 | tf_op jit(solution)/shard_map/while/body/eval_jaxpr/ppermute | solution.py:12
  104.1 12.9 %collective-permute-done = bf16[2,768,256]{2,1,0:T(8,128)(2,1)S(1)} collective-permute-done((bf16[2,768,256]{2,1,0:T(8,128)(2,1)S(1)}, bf16[2,768,256]{2,1,0:T(8,128)(2,1)S(1)}, u32[]{:S(2)}, u32[]{:S(2)}) %collective-permute-start) | collective-permute-done | bytes 786464 | tf_op jit(solution)/shard_map/while/body/eval_jaxpr/ppermute | solution.py:12
  118.9 12.9 %collective-permute-done = bf16[2,768,256]{2,1,0:T(8,128)(2,1)S(1)} collective-permute-done((bf16[2,768,256]{2,1,0:T(8,128)(2,1)S(1)}, bf16[2,768,256]{2,1,0:T(8,128)(2,1)S(1)}, u32[]{:S(2)}, u32[]{:S(2)}) %collective-permute-start) | collective-permute-done | bytes 786464 | tf_op jit(solution)/shard_map/while/body/eval_jaxpr/ppermute | solution.py:12
  133.8 12.9 %collective-permute-done = bf16[2,768,256]{2,1,0:T(8,128)(2,1)S(1)} collective-permute-done((bf16[2,768,256]{2,1,0:T(8,128)(2,1)S(1)}, bf16[2,768,256]{2,1,0:T(8,128)(2,1)S(1)}, u32[]{:S(2)}, u32[]{:S(2)}) %collective-permute-start) | collective-permute-done | bytes 786464 | tf_op jit(solution)/shard_map/while/body/eval_jaxpr/ppermute | solution.py:12
  149.2 12.4 %collective-permute-done = bf16[2,768,256]{2,1,0:T(8,128)(2,1)S(1)} collective-permute-done((bf16[2,768,256]{2,1,0:T(8,128)(2,1)S(1)}, bf16[2,768,256]{2,1,0:T(8,128)(2,1)S(1)}, u32[]{:S(2)}, u32[]{:S(2)}) %collective-permute-start) | collective-permute-done | bytes 786464 | tf_op jit(solution)/shard_map/while/body/eval_jaxpr/ppermute | solution.py:12
  227.9 13.4 %collective-permute-done = bf16[2,768,256]{2,1,0:T(8,128)(2,1)S(1)} collective-permute-done((bf16[2,768,256]{2,1,0:T(8,128)(2,1)S(1)}, bf16[2,768,256]{2,1,0:T(8,128)(2,1)S(1)}, u32[]{:S(2)}, u32[]{:S(2)}) %collective-permute-start) | collective-permute-done | bytes 786464 | tf_op jit(solution)/shard_map/while/body/eval_jaxpr/ppermute | solution.py:12
  243.6 14.6 %collective-permute-done = bf16[2,768,256]{2,1,0:T(8,128)(2,1)S(1)} collective-permute-done((bf16[2,768,256]{2,1,0:T(8,128)(2,1)S(1)}, bf16[2,768,256]{2,1,0:T(8,128)(2,1)S(1)}, u32[]{:S(2)}, u32[]{:S(2)}) %collective-permute-start) | collective-permute-done | bytes 786464 | tf_op jit(solution)/shard_map/while/body/eval_jaxpr/ppermute | solution.py:12
  260.2 15.0 %collective-permute-done = bf16[2,768,256]{2,1,0:T(8,128)(2,1)S(1)} collective-permute-done((bf16[2,768,256]{2,1,0:T(8,128)(2,1)S(1)}, bf16[2,768,256]{2,1,0:T(8,128)(2,1)S(1)}, u32[]{:S(2)}, u32[]{:S(2)}) %collective-permute-start) | collective-permute-done | bytes 786464 | tf_op jit(solution)/shard_map/while/body/eval_jaxpr/ppermute | solution.py:12
  277.1 15.0 %collective-permute-done = bf16[2,768,256]{2,1,0:T(8,128)(2,1)S(1)} collective-permute-done((bf16[2,768,256]{2,1,0:T(8,128)(2,1)S(1)}, bf16[2,768,256]{2,1,0:T(8,128)(2,1)S(1)}, u32[]{:S(2)}, u32[]{:S(2)}) %collective-permute-start) | collective-permute-done | bytes 786464 | tf_op jit(solution)/shard_map/while/body/eval_jaxpr/ppermute | solution.py:12
  294.1 15.0 %collective-permute-done = bf16[2,768,256]{2,1,0:T(8,128)(2,1)S(1)} collective-permute-done((bf16[2,768,256]{2,1,0:T(8,128)(2,1)S(1)}, bf16[2,768,256]{2,1,0:T(8,128)(2,1)S(1)}, u32[]{:S(2)}, u32[]{:S(2)}) %collective-permute-start) | collective-permute-done | bytes 786464 | tf_op jit(solution)/shard_map/while/body/eval_jaxpr/ppermute | solution.py:12
  311.1 15.0 %collective-permute-done = bf16[2,768,256]{2,1,0:T(8,128)(2,1)S(1)} collective-permute-done((bf16[2,768,256]{2,1,0:T(8,128)(2,1)S(1)}, bf16[2,768,256]{2,1,0:T(8,128)(2,1)S(1)}, u32[]{:S(2)}, u32[]{:S(2)}) %collective-permute-start) | collective-permute-done | bytes 786464 | tf_op jit(solution)/shard_map/while/body/eval_jaxpr/ppermute | solution.py:12
  328.0 15.0 %collective-permute-done = bf16[2,768,256]{2,1,0:T(8,128)(2,1)S(1)} collective-permute-done((bf16[2,768,256]{2,1,0:T(8,128)(2,1)S(1)}, bf16[2,768,256]{2,1,0:T(8,128)(2,1)S(1)}, u32[]{:S(2)}, u32[]{:S(2)}) %collective-permute-start) | collective-permute-done | bytes 786464 | tf_op jit(solution)/shard_map/while/body/eval_jaxpr/ppermute | solution.py:12
  345.0 15.1 %collective-permute-done = bf16[2,768,256]{2,1,0:T(8,128)(2,1)S(1)} collective-permute-done((bf16[2,768,256]{2,1,0:T(8,128)(2,1)S(1)}, bf16[2,768,256]{2,1,0:T(8,128)(2,1)S(1)}, u32[]{:S(2)}, u32[]{:S(2)}) %collective-permute-start) | collective-permute-done | bytes 786464 | tf_op jit(solution)/shard_map/while/body/eval_jaxpr/ppermute | solution.py:12
  362.0 15.0 %collective-permute-done = bf16[2,768,256]{2,1,0:T(8,128)(2,1)S(1)} collective-permute-done((bf16[2,768,256]{2,1,0:T(8,128)(2,1)S(1)}, bf16[2,768,256]{2,1,0:T(8,128)(2,1)S(1)}, u32[]{:S(2)}, u32[]{:S(2)}) %collective-permute-start) | collective-permute-done | bytes 786464 | tf_op jit(solution)/shard_map/while/body/eval_jaxpr/ppermute | solution.py:12
  378.9 15.0 %collective-permute-done = bf16[2,768,256]{2,1,0:T(8,128)(2,1)S(1)} collective-permute-done((bf16[2,768,256]{2,1,0:T(8,128)(2,1)S(1)}, bf16[2,768,256]{2,1,0:T(8,128)(2,1)S(1)}, u32[]{:S(2)}, u32[]{:S(2)}) %collective-permute-start) | collective-permute-done | bytes 786464 | tf_op jit(solution)/shard_map/while/body/eval_jaxpr/ppermute | solution.py:12
  395.8 15.0 %collective-permute-done = bf16[2,768,256]{2,1,0:T(8,128)(2,1)S(1)} collective-permute-done((bf16[2,768,256]{2,1,0:T(8,128)(2,1)S(1)}, bf16[2,768,256]{2,1,0:T(8,128)(2,1)S(1)}, u32[]{:S(2)}, u32[]{:S(2)}) %collective-permute-start) | collective-permute-done | bytes 786464 | tf_op jit(solution)/shard_map/while/body/eval_jaxpr/ppermute | solution.py:12
  412.8 15.0 %collective-permute-done = bf16[2,768,256]{2,1,0:T(8,128)(2,1)S(1)} collective-permute-done((bf16[2,768,256]{2,1,0:T(8,128)(2,1)S(1)}, bf16[2,768,256]{2,1,0:T(8,128)(2,1)S(1)}, u32[]{:S(2)}, u32[]{:S(2)}) %collective-permute-start) | collective-permute-done | bytes 786464 | tf_op jit(solution)/shard_map/while/body/eval_jaxpr/ppermute | solution.py:12
  429.8 15.0 %collective-permute-done = bf16[2,768,256]{2,1,0:T(8,128)(2,1)S(1)} collective-permute-done((bf16[2,768,256]{2,1,0:T(8,128)(2,1)S(1)}, bf16[2,768,256]{2,1,0:T(8,128)(2,1)S(1)}, u32[]{:S(2)}, u32[]{:S(2)}) %collective-permute-start) | collective-permute-done | bytes 786464 | tf_op jit(solution)/shard_map/while/body/eval_jaxpr/ppermute | solution.py:12
  446.7 15.0 %collective-permute-done = bf16[2,768,256]{2,1,0:T(8,128)(2,1)S(1)} collective-permute-done((bf16[2,768,256]{2,1,0:T(8,128)(2,1)S(1)}, bf16[2,768,256]{2,1,0:T(8,128)(2,1)S(1)}, u32[]{:S(2)}, u32[]{:S(2)}) %collective-permute-start) | collective-permute-done | bytes 786464 | tf_op jit(solution)/shard_map/while/body/eval_jaxpr/ppermute | solution.py:12
  463.7 15.0 %collective-permute-done = bf16[2,768,256]{2,1,0:T(8,128)(2,1)S(1)} collective-permute-done((bf16[2,768,256]{2,1,0:T(8,128)(2,1)S(1)}, bf16[2,768,256]{2,1,0:T(8,128)(2,1)S(1)}, u32[]{:S(2)}, u32[]{:S(2)}) %collective-permute-start) | collective-permute-done | bytes 786464 | tf_op jit(solution)/shard_map/while/body/eval_jaxpr/ppermute | solution.py:12
  480.6 15.0 %collective-permute-done = bf16[2,768,256]{2,1,0:T(8,128)(2,1)S(1)} collective-permute-done((bf16[2,768,256]{2,1,0:T(8,128)(2,1)S(1)}, bf16[2,768,256]{2,1,0:T(8,128)(2,1)S(1)}, u32[]{:S(2)}, u32[]{:S(2)}) %collective-permute-start) | collective-permute-done | bytes 786464 | tf_op jit(solution)/shard_map/while/body/eval_jaxpr/ppermute | solution.py:12
  497.6 15.0 %collective-permute-done = bf16[2,768,256]{2,1,0:T(8,128)(2,1)S(1)} collective-permute-done((bf16[2,768,256]{2,1,0:T(8,128)(2,1)S(1)}, bf16[2,768,256]{2,1,0:T(8,128)(2,1)S(1)}, u32[]{:S(2)}, u32[]{:S(2)}) %collective-permute-start) | collective-permute-done | bytes 786464 | tf_op jit(solution)/shard_map/while/body/eval_jaxpr/ppermute | solution.py:12
  514.6 15.0 %collective-permute-done = bf16[2,768,256]{2,1,0:T(8,128)(2,1)S(1)} collective-permute-done((bf16[2,768,256]{2,1,0:T(8,128)(2,1)S(1)}, bf16[2,768,256]{2,1,0:T(8,128)(2,1)S(1)}, u32[]{:S(2)}, u32[]{:S(2)}) %collective-permute-start) | collective-permute-done | bytes 786464 | tf_op jit(solution)/shard_map/while/body/eval_jaxpr/ppermute | solution.py:12
  531.5 15.0 %collective-permute-done = bf16[2,768,256]{2,1,0:T(8,128)(2,1)S(1)} collective-permute-done((bf16[2,768,256]{2,1,0:T(8,128)(2,1)S(1)}, bf16[2,768,256]{2,1,0:T(8,128)(2,1)S(1)}, u32[]{:S(2)}, u32[]{:S(2)}) %collective-permute-start) | collective-permute-done | bytes 786464 | tf_op jit(solution)/shard_map/while/body/eval_jaxpr/ppermute | solution.py:12
  548.4 15.0 %collective-permute-done = bf16[2,768,256]{2,1,0:T(8,128)(2,1)S(1)} collective-permute-done((bf16[2,768,256]{2,1,0:T(8,128)(2,1)S(1)}, bf16[2,768,256]{2,1,0:T(8,128)(2,1)S(1)}, u32[]{:S(2)}, u32[]{:S(2)}) %collective-permute-start) | collective-permute-done | bytes 786464 | tf_op jit(solution)/shard_map/while/body/eval_jaxpr/ppermute | solution.py:12
  565.4 15.0 %collective-permute-done = bf16[2,768,256]{2,1,0:T(8,128)(2,1)S(1)} collective-permute-done((bf16[2,768,256]{2,1,0:T(8,128)(2,1)S(1)}, bf16[2,768,256]{2,1,0:T(8,128)(2,1)S(1)}, u32[]{:S(2)}, u32[]{:S(2)}) %collective-permute-start) | collective-permute-done | bytes 786464 | tf_op jit(solution)/shard_map/while/body/eval_jaxpr/ppermute | solution.py:12
  582.4 15.0 %collective-permute-done = bf16[2,768,256]{2,1,0:T(8,128)(2,1)S(1)} collective-permute-done((bf16[2,768,256]{2,1,0:T(8,128)(2,1)S(1)}, bf16[2,768,256]{2,1,0:T(8,128)(2,1)S(1)}, u32[]{:S(2)}, u32[]{:S(2)}) %collective-permute-start) | collective-permute-done | bytes 786464 | tf_op jit(solution)/shard_map/while/body/eval_jaxpr/ppermute | solution.py:12
  610.3 13.0 %gather_fusion.1 = bf16[3072,256]{1,0:T(8,128)(2,1)} fusion(bf16[6144,256]{1,0:T(8,128)(2,1)S(1)} %reshape.185, s32[3072]{0:T(1024)S(1)} %broadcast_clamp_fusion), kind=kCustom, calls=%fused_computation.1 | custom fusion | bytes 3158016 | tf_op jit(solution)/shard_map/gather | solution.py:76
  626.5 60.5 %all-gather.2.cloned.1.call-done = bf16[384,2048]{1,0:T(8,128)(2,1)} async-done(((bf16[384,256]{1,0:T(8,128)(2,1)}), bf16[384,2048]{1,0:T(8,128)(2,1)}) %all-gather.2.cloned.1.call-update) | async-done | bytes 1572880 | tf_op jit(solution)/shard_map/all_gather | solution.py:79
  (126 shorter events, 166.5 us)
Async XLA Ops:
  6.5 680.5 %all-gather.2.cloned.1.call-start = ((), (), s32[]{:S(2)}) async-start(), calls=%async_computation | async-start | bytes 1769472 | tf_op jit(solution)/shard_map/all_gather | solution.py:79
  89.2 12.9 %collective-permute-start = (bf16[2,768,256]{2,1,0:T(8,128)(2,1)S(1)}, bf16[2,768,256]{2,1,0:T(8,128)(2,1)S(1)}, u32[]{:S(2)}, u32[]{:S(2)}) collective-permute-start(bf16[2,768,256]{2,1,0:T(8,128)(2,1)S(1)} %get-tuple-element.200), channel_id=1, source_target_pairs={{0,1},{1,2},{2,3},{3,4},{4,5},{5,6},{6,7},{7,8},{8,9},{9,10},{10,1... | collective-permute-start | bytes 2359304 | tf_op jit(solution)/shard_map/while/body/eval_jaxpr/ppermute | solution.py:12
  104.1 12.9 %collective-permute-start = (bf16[2,768,256]{2,1,0:T(8,128)(2,1)S(1)}, bf16[2,768,256]{2,1,0:T(8,128)(2,1)S(1)}, u32[]{:S(2)}, u32[]{:S(2)}) collective-permute-start(bf16[2,768,256]{2,1,0:T(8,128)(2,1)S(1)} %get-tuple-element.200), channel_id=1, source_target_pairs={{0,1},{1,2},{2,3},{3,4},{4,5},{5,6},{6,7},{7,8},{8,9},{9,10},{10,1... | collective-permute-start | bytes 2359304 | tf_op jit(solution)/shard_map/while/body/eval_jaxpr/ppermute | solution.py:12
  118.9 12.9 %collective-permute-start = (bf16[2,768,256]{2,1,0:T(8,128)(2,1)S(1)}, bf16[2,768,256]{2,1,0:T(8,128)(2,1)S(1)}, u32[]{:S(2)}, u32[]{:S(2)}) collective-permute-start(bf16[2,768,256]{2,1,0:T(8,128)(2,1)S(1)} %get-tuple-element.200), channel_id=1, source_target_pairs={{0,1},{1,2},{2,3},{3,4},{4,5},{5,6},{6,7},{7,8},{8,9},{9,10},{10,1... | collective-permute-start | bytes 2359304 | tf_op jit(solution)/shard_map/while/body/eval_jaxpr/ppermute | solution.py:12
  133.8 12.9 %collective-permute-start = (bf16[2,768,256]{2,1,0:T(8,128)(2,1)S(1)}, bf16[2,768,256]{2,1,0:T(8,128)(2,1)S(1)}, u32[]{:S(2)}, u32[]{:S(2)}) collective-permute-start(bf16[2,768,256]{2,1,0:T(8,128)(2,1)S(1)} %get-tuple-element.200), channel_id=1, source_target_pairs={{0,1},{1,2},{2,3},{3,4},{4,5},{5,6},{6,7},{7,8},{8,9},{9,10},{10,1... | collective-permute-start | bytes 2359304 | tf_op jit(solution)/shard_map/while/body/eval_jaxpr/ppermute | solution.py:12
  148.6 12.9 %collective-permute-start = (bf16[2,768,256]{2,1,0:T(8,128)(2,1)S(1)}, bf16[2,768,256]{2,1,0:T(8,128)(2,1)S(1)}, u32[]{:S(2)}, u32[]{:S(2)}) collective-permute-start(bf16[2,768,256]{2,1,0:T(8,128)(2,1)S(1)} %get-tuple-element.200), channel_id=1, source_target_pairs={{0,1},{1,2},{2,3},{3,4},{4,5},{5,6},{6,7},{7,8},{8,9},{9,10},{10,1... | collective-permute-start | bytes 2359304 | tf_op jit(solution)/shard_map/while/body/eval_jaxpr/ppermute | solution.py:12
  163.5 12.9 %collective-permute-start = (bf16[2,768,256]{2,1,0:T(8,128)(2,1)S(1)}, bf16[2,768,256]{2,1,0:T(8,128)(2,1)S(1)}, u32[]{:S(2)}, u32[]{:S(2)}) collective-permute-start(bf16[2,768,256]{2,1,0:T(8,128)(2,1)S(1)} %get-tuple-element.200), channel_id=1, source_target_pairs={{0,1},{1,2},{2,3},{3,4},{4,5},{5,6},{6,7},{7,8},{8,9},{9,10},{10,1... | collective-permute-start | bytes 2359304 | tf_op jit(solution)/shard_map/while/body/eval_jaxpr/ppermute | solution.py:12
  178.3 12.9 %collective-permute-start = (bf16[2,768,256]{2,1,0:T(8,128)(2,1)S(1)}, bf16[2,768,256]{2,1,0:T(8,128)(2,1)S(1)}, u32[]{:S(2)}, u32[]{:S(2)}) collective-permute-start(bf16[2,768,256]{2,1,0:T(8,128)(2,1)S(1)} %get-tuple-element.200), channel_id=1, source_target_pairs={{0,1},{1,2},{2,3},{3,4},{4,5},{5,6},{6,7},{7,8},{8,9},{9,10},{10,1... | collective-permute-start | bytes 2359304 | tf_op jit(solution)/shard_map/while/body/eval_jaxpr/ppermute | solution.py:12
  193.2 14.2 %collective-permute-start = (bf16[2,768,256]{2,1,0:T(8,128)(2,1)S(1)}, bf16[2,768,256]{2,1,0:T(8,128)(2,1)S(1)}, u32[]{:S(2)}, u32[]{:S(2)}) collective-permute-start(bf16[2,768,256]{2,1,0:T(8,128)(2,1)S(1)} %get-tuple-element.200), channel_id=1, source_target_pairs={{0,1},{1,2},{2,3},{3,4},{4,5},{5,6},{6,7},{7,8},{8,9},{9,10},{10,1... | collective-permute-start | bytes 2359304 | tf_op jit(solution)/shard_map/while/body/eval_jaxpr/ppermute | solution.py:12
  209.3 15.0 %collective-permute-start = (bf16[2,768,256]{2,1,0:T(8,128)(2,1)S(1)}, bf16[2,768,256]{2,1,0:T(8,128)(2,1)S(1)}, u32[]{:S(2)}, u32[]{:S(2)}) collective-permute-start(bf16[2,768,256]{2,1,0:T(8,128)(2,1)S(1)} %get-tuple-element.200), channel_id=1, source_target_pairs={{0,1},{1,2},{2,3},{3,4},{4,5},{5,6},{6,7},{7,8},{8,9},{9,10},{10,1... | collective-permute-start | bytes 2359304 | tf_op jit(solution)/shard_map/while/body/eval_jaxpr/ppermute | solution.py:12
  226.3 15.0 %collective-permute-start = (bf16[2,768,256]{2,1,0:T(8,128)(2,1)S(1)}, bf16[2,768,256]{2,1,0:T(8,128)(2,1)S(1)}, u32[]{:S(2)}, u32[]{:S(2)}) collective-permute-start(bf16[2,768,256]{2,1,0:T(8,128)(2,1)S(1)} %get-tuple-element.200), channel_id=1, source_target_pairs={{0,1},{1,2},{2,3},{3,4},{4,5},{5,6},{6,7},{7,8},{8,9},{9,10},{10,1... | collective-permute-start | bytes 2359304 | tf_op jit(solution)/shard_map/while/body/eval_jaxpr/ppermute | solution.py:12
  243.2 15.1 %collective-permute-start = (bf16[2,768,256]{2,1,0:T(8,128)(2,1)S(1)}, bf16[2,768,256]{2,1,0:T(8,128)(2,1)S(1)}, u32[]{:S(2)}, u32[]{:S(2)}) collective-permute-start(bf16[2,768,256]{2,1,0:T(8,128)(2,1)S(1)} %get-tuple-element.200), channel_id=1, source_target_pairs={{0,1},{1,2},{2,3},{3,4},{4,5},{5,6},{6,7},{7,8},{8,9},{9,10},{10,1... | collective-permute-start | bytes 2359304 | tf_op jit(solution)/shard_map/while/body/eval_jaxpr/ppermute | solution.py:12
  260.2 15.0 %collective-permute-start = (bf16[2,768,256]{2,1,0:T(8,128)(2,1)S(1)}, bf16[2,768,256]{2,1,0:T(8,128)(2,1)S(1)}, u32[]{:S(2)}, u32[]{:S(2)}) collective-permute-start(bf16[2,768,256]{2,1,0:T(8,128)(2,1)S(1)} %get-tuple-element.200), channel_id=1, source_target_pairs={{0,1},{1,2},{2,3},{3,4},{4,5},{5,6},{6,7},{7,8},{8,9},{9,10},{10,1... | collective-permute-start | bytes 2359304 | tf_op jit(solution)/shard_map/while/body/eval_jaxpr/ppermute | solution.py:12
  277.1 15.0 %collective-permute-start = (bf16[2,768,256]{2,1,0:T(8,128)(2,1)S(1)}, bf16[2,768,256]{2,1,0:T(8,128)(2,1)S(1)}, u32[]{:S(2)}, u32[]{:S(2)}) collective-permute-start(bf16[2,768,256]{2,1,0:T(8,128)(2,1)S(1)} %get-tuple-element.200), channel_id=1, source_target_pairs={{0,1},{1,2},{2,3},{3,4},{4,5},{5,6},{6,7},{7,8},{8,9},{9,10},{10,1... | collective-permute-start | bytes 2359304 | tf_op jit(solution)/shard_map/while/body/eval_jaxpr/ppermute | solution.py:12
  294.1 15.1 %collective-permute-start = (bf16[2,768,256]{2,1,0:T(8,128)(2,1)S(1)}, bf16[2,768,256]{2,1,0:T(8,128)(2,1)S(1)}, u32[]{:S(2)}, u32[]{:S(2)}) collective-permute-start(bf16[2,768,256]{2,1,0:T(8,128)(2,1)S(1)} %get-tuple-element.200), channel_id=1, source_target_pairs={{0,1},{1,2},{2,3},{3,4},{4,5},{5,6},{6,7},{7,8},{8,9},{9,10},{10,1... | collective-permute-start | bytes 2359304 | tf_op jit(solution)/shard_map/while/body/eval_jaxpr/ppermute | solution.py:12
  311.1 15.0 %collective-permute-start = (bf16[2,768,256]{2,1,0:T(8,128)(2,1)S(1)}, bf16[2,768,256]{2,1,0:T(8,128)(2,1)S(1)}, u32[]{:S(2)}, u32[]{:S(2)}) collective-permute-start(bf16[2,768,256]{2,1,0:T(8,128)(2,1)S(1)} %get-tuple-element.200), channel_id=1, source_target_pairs={{0,1},{1,2},{2,3},{3,4},{4,5},{5,6},{6,7},{7,8},{8,9},{9,10},{10,1... | collective-permute-start | bytes 2359304 | tf_op jit(solution)/shard_map/while/body/eval_jaxpr/ppermute | solution.py:12
  328.0 15.0 %collective-permute-start = (bf16[2,768,256]{2,1,0:T(8,128)(2,1)S(1)}, bf16[2,768,256]{2,1,0:T(8,128)(2,1)S(1)}, u32[]{:S(2)}, u32[]{:S(2)}) collective-permute-start(bf16[2,768,256]{2,1,0:T(8,128)(2,1)S(1)} %get-tuple-element.200), channel_id=1, source_target_pairs={{0,1},{1,2},{2,3},{3,4},{4,5},{5,6},{6,7},{7,8},{8,9},{9,10},{10,1... | collective-permute-start | bytes 2359304 | tf_op jit(solution)/shard_map/while/body/eval_jaxpr/ppermute | solution.py:12
  345.0 15.1 %collective-permute-start = (bf16[2,768,256]{2,1,0:T(8,128)(2,1)S(1)}, bf16[2,768,256]{2,1,0:T(8,128)(2,1)S(1)}, u32[]{:S(2)}, u32[]{:S(2)}) collective-permute-start(bf16[2,768,256]{2,1,0:T(8,128)(2,1)S(1)} %get-tuple-element.200), channel_id=1, source_target_pairs={{0,1},{1,2},{2,3},{3,4},{4,5},{5,6},{6,7},{7,8},{8,9},{9,10},{10,1... | collective-permute-start | bytes 2359304 | tf_op jit(solution)/shard_map/while/body/eval_jaxpr/ppermute | solution.py:12
  362.0 15.0 %collective-permute-start = (bf16[2,768,256]{2,1,0:T(8,128)(2,1)S(1)}, bf16[2,768,256]{2,1,0:T(8,128)(2,1)S(1)}, u32[]{:S(2)}, u32[]{:S(2)}) collective-permute-start(bf16[2,768,256]{2,1,0:T(8,128)(2,1)S(1)} %get-tuple-element.200), channel_id=1, source_target_pairs={{0,1},{1,2},{2,3},{3,4},{4,5},{5,6},{6,7},{7,8},{8,9},{9,10},{10,1... | collective-permute-start | bytes 2359304 | tf_op jit(solution)/shard_map/while/body/eval_jaxpr/ppermute | solution.py:12
  378.9 15.0 %collective-permute-start = (bf16[2,768,256]{2,1,0:T(8,128)(2,1)S(1)}, bf16[2,768,256]{2,1,0:T(8,128)(2,1)S(1)}, u32[]{:S(2)}, u32[]{:S(2)}) collective-permute-start(bf16[2,768,256]{2,1,0:T(8,128)(2,1)S(1)} %get-tuple-element.200), channel_id=1, source_target_pairs={{0,1},{1,2},{2,3},{3,4},{4,5},{5,6},{6,7},{7,8},{8,9},{9,10},{10,1... | collective-permute-start | bytes 2359304 | tf_op jit(solution)/shard_map/while/body/eval_jaxpr/ppermute | solution.py:12
  395.8 15.0 %collective-permute-start = (bf16[2,768,256]{2,1,0:T(8,128)(2,1)S(1)}, bf16[2,768,256]{2,1,0:T(8,128)(2,1)S(1)}, u32[]{:S(2)}, u32[]{:S(2)}) collective-permute-start(bf16[2,768,256]{2,1,0:T(8,128)(2,1)S(1)} %get-tuple-element.200), channel_id=1, source_target_pairs={{0,1},{1,2},{2,3},{3,4},{4,5},{5,6},{6,7},{7,8},{8,9},{9,10},{10,1... | collective-permute-start | bytes 2359304 | tf_op jit(solution)/shard_map/while/body/eval_jaxpr/ppermute | solution.py:12
  412.8 15.0 %collective-permute-start = (bf16[2,768,256]{2,1,0:T(8,128)(2,1)S(1)}, bf16[2,768,256]{2,1,0:T(8,128)(2,1)S(1)}, u32[]{:S(2)}, u32[]{:S(2)}) collective-permute-start(bf16[2,768,256]{2,1,0:T(8,128)(2,1)S(1)} %get-tuple-element.200), channel_id=1, source_target_pairs={{0,1},{1,2},{2,3},{3,4},{4,5},{5,6},{6,7},{7,8},{8,9},{9,10},{10,1... | collective-permute-start | bytes 2359304 | tf_op jit(solution)/shard_map/while/body/eval_jaxpr/ppermute | solution.py:12
  429.8 15.0 %collective-permute-start = (bf16[2,768,256]{2,1,0:T(8,128)(2,1)S(1)}, bf16[2,768,256]{2,1,0:T(8,128)(2,1)S(1)}, u32[]{:S(2)}, u32[]{:S(2)}) collective-permute-start(bf16[2,768,256]{2,1,0:T(8,128)(2,1)S(1)} %get-tuple-element.200), channel_id=1, source_target_pairs={{0,1},{1,2},{2,3},{3,4},{4,5},{5,6},{6,7},{7,8},{8,9},{9,10},{10,1... | collective-permute-start | bytes 2359304 | tf_op jit(solution)/shard_map/while/body/eval_jaxpr/ppermute | solution.py:12
  446.7 15.0 %collective-permute-start = (bf16[2,768,256]{2,1,0:T(8,128)(2,1)S(1)}, bf16[2,768,256]{2,1,0:T(8,128)(2,1)S(1)}, u32[]{:S(2)}, u32[]{:S(2)}) collective-permute-start(bf16[2,768,256]{2,1,0:T(8,128)(2,1)S(1)} %get-tuple-element.200), channel_id=1, source_target_pairs={{0,1},{1,2},{2,3},{3,4},{4,5},{5,6},{6,7},{7,8},{8,9},{9,10},{10,1... | collective-permute-start | bytes 2359304 | tf_op jit(solution)/shard_map/while/body/eval_jaxpr/ppermute | solution.py:12
  463.7 15.0 %collective-permute-start = (bf16[2,768,256]{2,1,0:T(8,128)(2,1)S(1)}, bf16[2,768,256]{2,1,0:T(8,128)(2,1)S(1)}, u32[]{:S(2)}, u32[]{:S(2)}) collective-permute-start(bf16[2,768,256]{2,1,0:T(8,128)(2,1)S(1)} %get-tuple-element.200), channel_id=1, source_target_pairs={{0,1},{1,2},{2,3},{3,4},{4,5},{5,6},{6,7},{7,8},{8,9},{9,10},{10,1... | collective-permute-start | bytes 2359304 | tf_op jit(solution)/shard_map/while/body/eval_jaxpr/ppermute | solution.py:12
  480.6 15.0 %collective-permute-start = (bf16[2,768,256]{2,1,0:T(8,128)(2,1)S(1)}, bf16[2,768,256]{2,1,0:T(8,128)(2,1)S(1)}, u32[]{:S(2)}, u32[]{:S(2)}) collective-permute-start(bf16[2,768,256]{2,1,0:T(8,128)(2,1)S(1)} %get-tuple-element.200), channel_id=1, source_target_pairs={{0,1},{1,2},{2,3},{3,4},{4,5},{5,6},{6,7},{7,8},{8,9},{9,10},{10,1... | collective-permute-start | bytes 2359304 | tf_op jit(solution)/shard_map/while/body/eval_jaxpr/ppermute | solution.py:12
  497.6 15.0 %collective-permute-start = (bf16[2,768,256]{2,1,0:T(8,128)(2,1)S(1)}, bf16[2,768,256]{2,1,0:T(8,128)(2,1)S(1)}, u32[]{:S(2)}, u32[]{:S(2)}) collective-permute-start(bf16[2,768,256]{2,1,0:T(8,128)(2,1)S(1)} %get-tuple-element.200), channel_id=1, source_target_pairs={{0,1},{1,2},{2,3},{3,4},{4,5},{5,6},{6,7},{7,8},{8,9},{9,10},{10,1... | collective-permute-start | bytes 2359304 | tf_op jit(solution)/shard_map/while/body/eval_jaxpr/ppermute | solution.py:12
  514.5 15.0 %collective-permute-start = (bf16[2,768,256]{2,1,0:T(8,128)(2,1)S(1)}, bf16[2,768,256]{2,1,0:T(8,128)(2,1)S(1)}, u32[]{:S(2)}, u32[]{:S(2)}) collective-permute-start(bf16[2,768,256]{2,1,0:T(8,128)(2,1)S(1)} %get-tuple-element.200), channel_id=1, source_target_pairs={{0,1},{1,2},{2,3},{3,4},{4,5},{5,6},{6,7},{7,8},{8,9},{9,10},{10,1... | collective-permute-start | bytes 2359304 | tf_op jit(solution)/shard_map/while/body/eval_jaxpr/ppermute | solution.py:12
  531.5 15.0 %collective-permute-start = (bf16[2,768,256]{2,1,0:T(8,128)(2,1)S(1)}, bf16[2,768,256]{2,1,0:T(8,128)(2,1)S(1)}, u32[]{:S(2)}, u32[]{:S(2)}) collective-permute-start(bf16[2,768,256]{2,1,0:T(8,128)(2,1)S(1)} %get-tuple-element.200), channel_id=1, source_target_pairs={{0,1},{1,2},{2,3},{3,4},{4,5},{5,6},{6,7},{7,8},{8,9},{9,10},{10,1... | collective-permute-start | bytes 2359304 | tf_op jit(solution)/shard_map/while/body/eval_jaxpr/ppermute | solution.py:12
  548.4 15.0 %collective-permute-start = (bf16[2,768,256]{2,1,0:T(8,128)(2,1)S(1)}, bf16[2,768,256]{2,1,0:T(8,128)(2,1)S(1)}, u32[]{:S(2)}, u32[]{:S(2)}) collective-permute-start(bf16[2,768,256]{2,1,0:T(8,128)(2,1)S(1)} %get-tuple-element.200), channel_id=1, source_target_pairs={{0,1},{1,2},{2,3},{3,4},{4,5},{5,6},{6,7},{7,8},{8,9},{9,10},{10,1... | collective-permute-start | bytes 2359304 | tf_op jit(solution)/shard_map/while/body/eval_jaxpr/ppermute | solution.py:12
  565.4 15.0 %collective-permute-start = (bf16[2,768,256]{2,1,0:T(8,128)(2,1)S(1)}, bf16[2,768,256]{2,1,0:T(8,128)(2,1)S(1)}, u32[]{:S(2)}, u32[]{:S(2)}) collective-permute-start(bf16[2,768,256]{2,1,0:T(8,128)(2,1)S(1)} %get-tuple-element.200), channel_id=1, source_target_pairs={{0,1},{1,2},{2,3},{3,4},{4,5},{5,6},{6,7},{7,8},{8,9},{9,10},{10,1... | collective-permute-start | bytes 2359304 | tf_op jit(solution)/shard_map/while/body/eval_jaxpr/ppermute | solution.py:12
  582.4 15.0 %collective-permute-start = (bf16[2,768,256]{2,1,0:T(8,128)(2,1)S(1)}, bf16[2,768,256]{2,1,0:T(8,128)(2,1)S(1)}, u32[]{:S(2)}, u32[]{:S(2)}) collective-permute-start(bf16[2,768,256]{2,1,0:T(8,128)(2,1)S(1)} %get-tuple-element.200), channel_id=1, source_target_pairs={{0,1},{1,2},{2,3},{3,4},{4,5},{5,6},{6,7},{7,8},{8,9},{9,10},{10,1... | collective-permute-start | bytes 2359304 | tf_op jit(solution)/shard_map/while/body/eval_jaxpr/ppermute | solution.py:12
  (2 other events, 5.7 us)
Sparse Core Ops, SparseCore 0:
  626.6 60.3 all-gather.1
where the time goes:
time: 699 us; the launch traced here: 697 us
  waiting for transfers between devices  498 us (71%)
  local copies, waits for them, and re-layouts  109 us (16%)
  matrix products  59.6 us (9%)
  between operations  13.5 us (2%)
  starting transfers between devices  12.4 us (2%)
    ppermute x31, waiting for transfers between devices, passed_along(): return lax.ppermute(value, axis, pairs)  438 us
    all_gather x1, waiting for transfers between devices, local(): return lax.all_gather(mixed_part, 'dp', axis=1, tiled=True)  60.5 us
    dot_general x32, matrix products, expert_products(): jnp.einsum('cef,efd->ced', picked, weights, preferred_element_type=jnp.fl...  59.2 us
    gather x1, local copies, waits for them, and re-layouts, local(): row_table[slot_table]  31 us
    reshape x2, local copies, waits for them, and re-layouts, local(): row_table[slot_table]  28.6 us
  transfers between devices with their start and end apart: 32, of which 32 were waited for; matrix products, arithmetic and copies ran while one was open for 0% of the time, Pallas kernels for 0%

commit v1 on v0

v1 whole, which is shorter than its diff:
```python
import functools

import jax
import jax.numpy as jnp
from jax import lax
from jax.experimental import pallas as pl
from jax.experimental.pallas import tpu as pltpu
from jax.sharding import PartitionSpec as P

MESH = pl.DeviceIdType.MESH
TOKENS = 384
TOP = 8
FF = 768
COLS = 256
BLOCK = 32
BLOCKS = TOKENS // BLOCK
ROUTES = BLOCK * TOP
HOPS = 7
SUBS = 6
SUB_ROWS = TOKENS * TOP // 4 // SUBS
OWN_BATCH = 16


def pick_rows(meta, hidden, picked, block, experts):
    ids = meta[pl.ds(block, 1), :]
    gates = meta[pl.ds(BLOCKS + block, 1), :]
    shape = (BLOCK, ROUTES)
    owner = lax.broadcasted_iota(jnp.int32, shape, 1) // TOP
    mine = owner == lax.broadcasted_iota(jnp.int32, shape, 0)
    names = jnp.where(mine, jnp.broadcast_to(ids, shape), -1.0)
    chosen = jnp.concatenate(
        [jnp.where(names == e, 1.0, 0.0).astype(jnp.bfloat16) for e in experts], axis=0
    )
    square = (ROUTES, ROUTES)
    diagonal = lax.broadcasted_iota(jnp.int32, square, 0) == lax.broadcasted_iota(
        jnp.int32, square, 1
    )
    column = jnp.sum(
        jnp.where(diagonal, jnp.broadcast_to(gates, square), 0.0), axis=1, keepdims=True
    )
    rows = hidden[pl.ds(pl.multiple_of(block * ROUTES, ROUTES), ROUTES), :]
    rows = (rows.astype(jnp.float32) * column).astype(jnp.bfloat16)
    result = jnp.dot(chosen, rows, preferred_element_type=jnp.float32).astype(jnp.bfloat16)
    for i in range(len(experts)):
        picked[pl.ds(pl.multiple_of(block * BLOCK, BLOCK), BLOCK), i * FF : (i + 1) * FF] = result[
            i * BLOCK : (i + 1) * BLOCK
        ]


def kernel(
    meta,
    hidden_in,
    weights_in,
    out,
    held,
    hidden,
    hidden_far,
    meta_far,
    picked,
    picked_far,
    total,
    total_far,
    sent,
    came,
    gathered,
    ring_send,
    ring_recv,
    core_send,
    core_recv,
    rows_send,
    rows_recv,
    end_send,
    end_recv,
    near_sem,
    out_sem,
):
    dp = lax.axis_index("dp")
    ex = lax.axis_index("expert")
    x, y_lo = lax.rem(dp, 4), dp // 4
    z, y_hi, core = ex // 4, lax.rem(ex // 2, 2), lax.rem(ex, 2)

    def device(x_, y_lo_, z_, y_hi_, core_):
        return (y_lo_ * 4 + lax.rem(x_ + 4, 4), lax.rem(z_ + 8, 8) * 4 + y_hi_ * 2 + core_)

    up, down = device(x, y_lo, z + 1, y_hi, core), device(x, y_lo, z - 1, y_hi, core)
    sibling = device(x, y_lo, z, y_hi, 1 - core)
    across = device(x, 1 - y_lo, z, 1 - y_hi, core)
    beside = device(x, 1 - y_lo, z, y_hi, core)
    right, left = device(x + 1, y_lo, z, y_hi, core), device(x - 1, y_lo, z, y_hi, core)
    opposite = device(x, y_lo, z, 1 - y_hi, core)

    def remote(src, dst, send_sem, recv_sem, to):
        return pltpu.make_async_remote_copy(
            src_ref=src,
            dst_ref=dst,
            send_sem=send_sem,
            recv_sem=recv_sem,
            device_id=to,
            device_id_type=MESH,
        )

    def place(first, count=1):
        return held.at[pl.ds(first * FF, count * FF)]

    def ring_copy(way, hop):
        if hop < 2:
            expert = hop if way == 0 else 1 - hop
            src = weights_in.at[pl.ds(expert * FF, FF)]
        else:
            src = place(4 * (hop - 1) + way)
        return remote(
            src,
            place(4 * (hop + 1) + way),
            ring_send.at[way, hop],
            ring_recv.at[way, hop],
            up if way == 0 else down,
        )

    def core_copy(group):
        src = weights_in if group == 0 else place(4 * group, 2)
        return remote(
            src, place(4 * group + 2, 2), core_send.at[group], core_recv.at[group], sibling
        )

    def experts_of(group):
        found = []
        for c in (core, 1 - core):
            for way in (0, 1):
                if group == 0:
                    where, which = z, way
                else:
                    hop = group - 1
                    step = 1 + hop // 2
                    where = lax.rem(z + (8 - step if way == 0 else step), 8)
                    which = hop % 2 if way == 0 else 1 - hop % 2
                found.append(((where * 2 + y_hi) * 2 + c) * 2 + which)
        return [e.astype(jnp.float32) for e in found]

    x_odd = lax.rem(x, 2)
    quarters = [
        x_odd * 2 + y_lo,
        x_odd * 2 + 1 - y_lo,
        (1 - x_odd) * 2 + y_lo,
        (1 - x_odd) * 2 + 1 - y_lo,
    ]

    def rows_of(quarter, sub):
        start = pl.multiple_of(quarter * (SUBS * SUB_ROWS) + sub * SUB_ROWS, SUB_ROWS)
        return pl.ds(start, SUB_ROWS)

    def rows_copy(kind, sub):
        quarter = quarters[(1, 0, 0, 1)[kind]]
        rows = rows_of(quarter, sub)
        src = (hidden_in if kind == 0 else hidden_far).at[rows]
        to = (across, beside, left, right)[kind]
        return remote(
            src, hidden_far.at[rows], rows_send.at[kind, sub], rows_recv.at[kind, sub], to
        )

    meta_copy = remote(meta, meta_far, end_send.at[0], end_recv.at[0], across)

    barrier = pltpu.get_barrier_semaphore()
    friends = (up, down, sibling, across, beside, right, left, opposite)
    for friend in friends:
        pl.semaphore_signal(barrier, inc=1, device_id=friend, device_id_type=MESH)
    near_hidden = pltpu.make_async_copy(hidden_in, hidden, near_sem.at[0])
    near_weights = pltpu.make_async_copy(weights_in, place(0, 2), near_sem.at[1])
    near_hidden.start()
    near_weights.start()
    pl.semaphore_wait(barrier, len(friends))

    for hop in (0, 1):
        for way in (0, 1):
            ring_copy(way, hop).start()
    meta_copy.start()
    for sub in range(SUBS):
        rows_copy(0, sub).start()
    core_copy(0).start()

    total[...] = jnp.zeros_like(total)
    total_far[...] = jnp.zeros_like(total_far)
    experts = [e for group in range(8) for e in experts_of(group)]

    def ring(hop):
        for way in (0, 1):
            ring_copy(way, hop).wait_recv()
            if hop + 2 < HOPS:
                ring_copy(way, hop + 2).start()
        core_copy(hop + 1).start()

    def from_across(sub):
        rows_copy(0, sub).wait_recv()
        rows_copy(1, sub).start()
        rows_copy(2, sub).start()

    def from_beside(sub):
        rows_copy(1, sub).wait_recv()
        rows_copy(3, sub).start()

    def pick_near(batch, first, count):
        @pl.loop(first, first + count)
        def _(block):
            pick_rows(
                meta, hidden, picked, block, experts[batch * OWN_BATCH : (batch + 1) * OWN_BATCH]
            )

    def pick_far(kind):
        @pl.loop(0, BLOCKS // 4)
        def _(i):
            pick_rows(
                meta_far, hidden_far, picked_far, quarters[kind] * (BLOCKS // 4) + i, experts
            )

    def multiply(acc, rows, column_group, group):
        acc[...] += jnp.dot(
            rows[:, column_group * 4 * FF : (column_group + 1) * 4 * FF],
            held[group * 4 * FF : (group + 1) * 4 * FF, :],
            preferred_element_type=jnp.float32,
        )

    def multiply_near(group):
        multiply(total, picked, group % 4, group)

    def multiply_far(group):
        multiply(total_far, picked_far, group, group)

    near_hidden.wait()
    pick_near(0, 0, 6)
    from_across(0)
    pick_near(0, 6, 6)
    from_across(1)
    ring(0)
    from_beside(0)
    near_weights.wait()
    core_copy(0).wait_recv()
    multiply_near(0)
    core_copy(1).wait_recv()
    multiply_near(1)
    from_across(2)
    from_beside(1)
    from_across(3)
    ring(1)
    from_beside(2)
    core_copy(2).wait_recv()
    multiply_near(2)
    from_across(4)
    from_beside(3)
    ring(2)
    from_across(5)
    core_copy(3).wait_recv()
    multiply_near(3)
    from_beside(4)
    pick_near(1, 0, 6)
    from_beside(5)
    pick_near(1, 6, 6)
    meta_copy.wait_recv()
    pick_far(0)
    pick_far(1)
    ring(3)
    for sub in range(SUBS):
        rows_copy(2, sub).wait_recv()
    pick_far(2)
    for sub in range(SUBS):
        rows_copy(3, sub).wait_recv()
    pick_far(3)
    core_copy(4).wait_recv()
    multiply_near(4)
    multiply_far(0)
    multiply_far(1)
    ring(4)
    multiply_far(2)
    multiply_far(3)
    multiply_far(4)
    core_copy(5).wait_recv()
    multiply_near(5)
    multiply_far(5)
    ring(5)
    core_copy(6).wait_recv()
    multiply_near(6)
    multiply_far(6)
    ring(6)
    core_copy(7).wait_recv()
    multiply_far(7)

    sent[...] = total_far[...].astype(jnp.bfloat16)
    sums = remote(sent, came, end_send.at[1], end_recv.at[1], opposite)
    sums.start()
    multiply_near(7)
    sums.wait_recv()
    gathered[dp] = (total[...] + came[...].astype(jnp.float32)).astype(jnp.bfloat16)

    half = TOKENS // 2
    dp_of = lambda x_, y_lo_: y_lo_ * 4 + lax.rem(x_ + 4, 4)

    def hand_on(number, block, to, rows=None):
        ref = gathered.at[block] if rows is None else gathered.at[block, pl.ds(rows, half)]
        return remote(ref, ref, end_send.at[number], end_recv.at[number], to)

    def write(number, block):
        return pltpu.make_async_copy(
            gathered.at[block],
            out.at[:, pl.ds(pl.multiple_of(block * COLS, COLS), COLS)],
            out_sem.at[number],
        )

    other = 1 - y_lo
    mine_up = hand_on(2, dp, beside)
    mine_right, mine_left = hand_on(3, dp, right), hand_on(4, dp, left)
    mine_right.start()
    mine_left.start()
    mine_up.start()
    write(0, dp).start()
    from_left, from_right = dp_of(x - 1, y_lo), dp_of(x + 1, y_lo)
    far_right, far_left = hand_on(5, from_left, right, 0), hand_on(6, from_right, left, half)
    mine_right.wait_recv()
    far_right.start()
    write(1, from_left).start()
    mine_left.wait_recv()
    far_left.start()
    write(2, from_right).start()
    mine_up.wait_recv()
    twin = dp_of(x, other)
    twin_right, twin_left = hand_on(7, twin, right), hand_on(8, twin, left)
    twin_right.start()
    twin_left.start()
    write(3, twin).start()
    far_right.wait_recv()
    far_left.wait_recv()
    far = dp_of(x + 2, y_lo)
    far_up = hand_on(9, far, beside)
    far_up.start()
    write(4, far).start()
    twin_right.wait_recv()
    write(5, dp_of(x - 1, other)).start()
    twin_left.wait_recv()
    write(6, dp_of(x + 1, other)).start()
    far_up.wait_recv()
    write(7, dp_of(x + 2, other)).start()

    for way in (0, 1):
        for hop in range(HOPS):
            ring_copy(way, hop).wait_send()
    for group in range(8):
        core_copy(group).wait_send()
    for kind in range(4):
        for sub in range(SUBS):
            rows_copy(kind, sub).wait_send()
    for copy in (
        meta_copy,
        sums,
        mine_up,
        mine_right,
        mine_left,
        far_right,
        far_left,
        twin_right,
        twin_left,
        far_up,
    ):
        copy.wait_send()
    blocks = (
        dp,
        from_left,
        from_right,
        twin,
        far,
        dp_of(x - 1, other),
        dp_of(x + 1, other),
        dp_of(x + 2, other),
    )
    for number, block in enumerate(blocks):
        write(number, block).wait()


def local(hidden, expert_ids, route_gates, down_weight):
    routes = TOKENS * TOP
    meta = jnp.concatenate(
        [
            expert_ids.astype(jnp.float32).reshape(BLOCKS, ROUTES),
            route_gates.reshape(BLOCKS, ROUTES),
        ],
        axis=0,
    )
    anywhere = pl.BlockSpec(memory_space=pl.ANY)
    dma = pltpu.SemaphoreType.DMA
    return pl.pallas_call(
        kernel,
        out_shape=jax.ShapeDtypeStruct((TOKENS, 8 * COLS), jnp.bfloat16),
        in_specs=[pl.BlockSpec(memory_space=pltpu.VMEM), anywhere, anywhere],
        out_specs=anywhere,
        scratch_shapes=[
            pltpu.VMEM((32 * FF, COLS), jnp.bfloat16),
            pltpu.VMEM((routes, FF), jnp.bfloat16),
            pltpu.VMEM((routes, FF), jnp.bfloat16),
            pltpu.VMEM((2 * BLOCKS, ROUTES), jnp.float32),
            pltpu.VMEM((TOKENS, OWN_BATCH * FF), jnp.bfloat16),
            pltpu.VMEM((TOKENS, 32 * FF), jnp.bfloat16),
            pltpu.VMEM((TOKENS, COLS), jnp.float32),
            pltpu.VMEM((TOKENS, COLS), jnp.float32),
            pltpu.VMEM((TOKENS, COLS), jnp.bfloat16),
            pltpu.VMEM((TOKENS, COLS), jnp.bfloat16),
            pltpu.VMEM((8, TOKENS, COLS), jnp.bfloat16),
            dma((2, HOPS)),
            dma((2, HOPS)),
            dma((8,)),
            dma((8,)),
            dma((4, SUBS)),
            dma((4, SUBS)),
            dma((10,)),
            dma((10,)),
            dma((2,)),
            dma((8,)),
        ],
        name="experts",
        compiler_params=pltpu.CompilerParams(
            collective_id=0, has_side_effects=True, vmem_limit_bytes=60 * 2**20
        ),
        cost_estimate=pl.CostEstimate(
            flops=2 * 2 * TOKENS * 32 * FF * COLS * 2,
            bytes_accessed=8 * 2**20,
            transcendentals=0,
        ),
    )(meta, hidden.reshape(routes, FF), down_weight.reshape(2 * FF, COLS))


def solution(mesh):
    placed = (
        P("expert", None, None),
        P("expert", None),
        P("expert", None),
        P("expert", None, "dp"),
    )
    return jax.shard_map(
        local, mesh=mesh, in_specs=placed, out_specs=P("expert", None), check_vma=False
    )
```

time: 699 us -> 104 us (0.15)
  waiting for transfers between devices: 498 us -> 0 us
  local copies, waits for them, and re-layouts: 109 us -> 3.95 us
  Pallas kernels: 0 us -> 97 us
  matrix products: 59.6 us -> 0 us
  between operations: 13.5 us -> 0.03 us
  starting transfers between devices: 12.4 us -> 0 us
    ppermute x31 -> x0, waiting for transfers between devices: 438 us -> none  [passed_along(): return lax.ppermute(value, axis, pairs)]
    pallas_call x0 -> x1, Pallas kernels: none -> 97 us  [local(): pl.pallas_call(kernel, out_shape=jax.ShapeDtypeStruct((TOKENS, 8 * COLS),...]
    all_gather x1 -> x0, waiting for transfers between devices: 60.5 us -> none  [local(): return lax.all_gather(mixed_part, 'dp', axis=1, tiled=True)]
    dot_general x33 -> x0, matrix products: 59.6 us -> none  [the longest x32 59.2 us: expert_products(): jnp.einsum('cef,efd->ced', picked, weights, preferred_element_type=jnp.fl...]
    gather x2 -> x0, local copies, waits for them, and re-layouts: 44.1 us -> none  [the longest x1 31 us: local(): row_table[slot_table]]
    reshape x4 -> x2, local copies, waits for them, and re-layouts: 32.8 us -> 0.27 us  [the longest x1 0.14 us: local(): expert_ids.astype(jnp.float32).reshape(BLOCKS, ROUTES)]
    ppermute x31 -> x0, starting transfers between devices: 12.4 us -> none  [passed_along(): return lax.ppermute(value, axis, pairs)]
    scatter x1 -> x0, local copies, waits for them, and re-layouts: 11.8 us -> none  [local(): jnp.full((expert_total * capacity,), route_total, jnp.int32).at[slot_index]]
  transfers between devices with their start and end apart: 32 -> 0, of which waited for: 32 -> 0; matrix products, arithmetic and copies ran while one was open for 0% -> 0% of each run, Pallas kernels for 0% -> 0%
where the time goes in v1:
time: 104 us; the launch traced here: 102 us
  Pallas kernels  97 us (93%)
  local copies, waits for them, and re-layouts  3.95 us (4%)
  other arithmetic  1.33 us (1%)
    pallas_call x1, Pallas kernels, local(): pl.pallas_call(kernel, out_shape=jax.ShapeDtypeStruct((TOKENS, 8 * COLS),...  97 us
    unnamed x2, local copies, waits for them, and re-layouts  3.56 us

profile of v1, /device:TPU:16, one launch (start us, length us, event | category | flops | bytes accessed | tf_op | source)
XLA Modules:
  0.0 102.3 jit_solution(13432036850187259953)
XLA Ops:
  0.0 0.7 convert_element_type.3
  0.7 0.1 copy.7
  0.8 0.1 reshape.12
  1.0 0.8 copy.8
  1.8 0.1 reshape.13
  2.0 0.6 pad_maximum_fusion.meta
  2.6 97.0 %experts.1 = bf16[384,2048]{1,0:T(8,128)(2,1)} custom-call(f32[24,256]{1,0:T(8,128)} %pad_maximum_fusion.meta, bf16[3072,768]{1,0:T(8,128)(2,1)} %bitcast.2, bf16[1536,256]{1,0:T(8,128)(2,1)} %bitcast.3), custom_call_target="tpu_custom_call" | custom-call | flops 19327352832 | bytes 8388608 | tf_op jit(solution)/shard_map/experts/pallas_call | solution.py:386
  99.6 2.7 %copy.10 = bf16[384,2048]{1,0:T(8,128)(2,1)} copy(bf16[384,2048]{1,0:T(8,128)(2,1)} %experts.1) | data formatting | bytes 3145728

commit v2 on v1

v2 whole, which is shorter than its diff:
```python
import functools

import jax
import jax.numpy as jnp
from jax import lax
from jax.experimental import pallas as pl
from jax.experimental.pallas import tpu as pltpu
from jax.sharding import PartitionSpec as P

MESH = pl.DeviceIdType.MESH
TOKENS = 384
TOP = 8
FF = 768
COLS = 256
BLOCK = 32
BLOCKS = TOKENS // BLOCK
ROUTES = BLOCK * TOP
HOPS = 7
QUARTER = TOKENS * TOP // 4
PIECES = (128, 128, 128, 128, 128, 64, 64)
SUBS = len(PIECES)
OWN_BATCH = 16
WHOLE = 5
LATE = HOPS - WHOLE
HALF = COLS // 2
STEPS = WHOLE + 2 * LATE
PARTS = ((0, 0, TOKENS), (1, 0, TOKENS // 2), (1, TOKENS // 2, TOKENS // 2))


def pick_rows(meta, hidden, picked, block, experts):
    ids = meta[pl.ds(block, 1), :]
    gates = meta[pl.ds(BLOCKS + block, 1), :]
    shape = (BLOCK, ROUTES)
    owner = lax.broadcasted_iota(jnp.int32, shape, 1) // TOP
    mine = owner == lax.broadcasted_iota(jnp.int32, shape, 0)
    names = jnp.where(mine, jnp.broadcast_to(ids, shape), -1.0)
    chosen = jnp.concatenate(
        [jnp.where(names == e, 1.0, 0.0).astype(jnp.bfloat16) for e in experts], axis=0
    )
    square = (ROUTES, ROUTES)
    diagonal = lax.broadcasted_iota(jnp.int32, square, 0) == lax.broadcasted_iota(
        jnp.int32, square, 1
    )
    column = jnp.sum(
        jnp.where(diagonal, jnp.broadcast_to(gates, square), 0.0), axis=1, keepdims=True
    )
    rows = hidden[pl.ds(pl.multiple_of(block * ROUTES, ROUTES), ROUTES), :]
    rows = (rows.astype(jnp.float32) * column).astype(jnp.bfloat16)
    result = jnp.dot(chosen, rows, preferred_element_type=jnp.float32).astype(jnp.bfloat16)
    for i in range(len(experts)):
        picked[pl.ds(pl.multiple_of(block * BLOCK, BLOCK), BLOCK), i * FF : (i + 1) * FF] = result[
            i * BLOCK : (i + 1) * BLOCK
        ]


def lay_out(ids, gates, meta):
    wide = (128, ROUTES)
    spread = (
        lax.rem(lax.broadcasted_iota(jnp.int32, (TOP, ROUTES), 1), TOP)
        == lax.broadcasted_iota(jnp.int32, (TOP, ROUTES), 0)
    ).astype(jnp.float32)
    mine = lax.broadcasted_iota(jnp.int32, wide, 1) // TOP == lax.rem(
        lax.broadcasted_iota(jnp.int32, wide, 0), BLOCK
    )
    for chunk in range(TOKENS // 128):
        columns = slice(chunk * 128, (chunk + 1) * 128)
        for first, part in ((0, ids[:, columns].astype(jnp.float32)), (BLOCKS, gates[:, columns])):
            full = lax.dot_general(
                part,
                spread,
                (((0,), (0,)), ((), ())),
                precision=lax.Precision.HIGHEST,
                preferred_element_type=jnp.float32,
            )
            full = jnp.where(mine, full, 0.0)
            for i in range(128 // BLOCK):
                row = first + chunk * (128 // BLOCK) + i
                meta[row : row + 1, :] = jnp.sum(
                    full[i * BLOCK : (i + 1) * BLOCK], axis=0, keepdims=True
                )


def kernel(
    ids_in,
    gates_in,
    hidden_in,
    weights_in,
    out,
    meta,
    held,
    late,
    hidden,
    hidden_far,
    meta_far,
    picked,
    picked_far,
    total,
    total_far,
    sent,
    came,
    gathered,
    ring_send,
    ring_recv,
    core_send,
    core_recv,
    rows_send,
    rows_recv,
    end_send,
    end_recv,
    meta_sem,
    near_sem,
    out_sem,
):
    dp = lax.axis_index("dp")
    ex = lax.axis_index("expert")
    x, y_lo = lax.rem(dp, 4), dp // 4
    z, y_hi, core = ex // 4, lax.rem(ex // 2, 2), lax.rem(ex, 2)

    def device(x_, y_lo_, z_, y_hi_, core_):
        return (y_lo_ * 4 + lax.rem(x_ + 4, 4), lax.rem(z_ + 8, 8) * 4 + y_hi_ * 2 + core_)

    up, down = device(x, y_lo, z + 1, y_hi, core), device(x, y_lo, z - 1, y_hi, core)
    sibling = device(x, y_lo, z, y_hi, 1 - core)
    across = device(x, 1 - y_lo, z, 1 - y_hi, core)
    beside = device(x, 1 - y_lo, z, y_hi, core)
    right, left = device(x + 1, y_lo, z, y_hi, core), device(x - 1, y_lo, z, y_hi, core)
    opposite = device(x, y_lo, z, 1 - y_hi, core)
    farther = device(x + 2, y_lo, z, y_hi, core)

    def remote(src, dst, send_sem, recv_sem, to):
        return pltpu.make_async_remote_copy(
            src_ref=src,
            dst_ref=dst,
            send_sem=send_sem,
            recv_sem=recv_sem,
            device_id=to,
            device_id_type=MESH,
        )

    def place(group, first, count):
        return held.at[pl.ds((4 * group + first) * FF, count * FF)]

    def late_place(half, group, first, count):
        return late.at[half, pl.ds((4 * (group - WHOLE - 1) + first) * FF, count * FF)]

    def hop_of(step):
        if step < WHOLE:
            return step, None
        return WHOLE + (step - WHOLE) % LATE, (step - WHOLE) // LATE

    def ring_copy(way, step):
        hop, half = hop_of(step)
        if hop < 2:
            src = weights_in.at[pl.ds((hop if way == 0 else 1 - hop) * FF, FF)]
        elif hop - 2 < WHOLE:
            src = place(hop - 1, way, 1)
            if half is not None:
                src = held.at[pl.ds((4 * (hop - 1) + way) * FF, FF), pl.ds(half * HALF, HALF)]
        else:
            src = late_place(half, hop - 1, way, 1)
        dst = place(hop + 1, way, 1) if half is None else late_place(half, hop + 1, way, 1)
        return remote(
            src,
            dst,
            ring_send.at[way, step],
            ring_recv.at[way, step],
            up if way == 0 else down,
        )

    def core_copy(number):
        if number == 0:
            src, dst = weights_in, place(0, 2, 2)
        else:
            hop, half = hop_of(number - 1)
            if half is None:
                src, dst = place(hop + 1, 0, 2), place(hop + 1, 2, 2)
            else:
                src, dst = late_place(half, hop + 1, 0, 2), late_place(half, hop + 1, 2, 2)
        return remote(src, dst, core_send.at[number], core_recv.at[number], sibling)

    def experts_of(group):
        found = []
        for c in (core, 1 - core):
            for way in (0, 1):
                if group == 0:
                    where, which = z, way
                else:
                    hop = group - 1
                    step = 1 + hop // 2
                    where = lax.rem(z + (8 - step if way == 0 else step), 8)
                    which = hop % 2 if way == 0 else 1 - hop % 2
                found.append(((where * 2 + y_hi) * 2 + c) * 2 + which)
        return [e.astype(jnp.float32) for e in found]

    x_odd = lax.rem(x, 2)
    quarters = [
        x_odd * 2 + y_lo,
        x_odd * 2 + 1 - y_lo,
        (1 - x_odd) * 2 + y_lo,
        (1 - x_odd) * 2 + 1 - y_lo,
    ]

    def rows_of(quarter, sub):
        start = pl.multiple_of(quarter * QUARTER + sum(PIECES[:sub]), 64)
        return pl.ds(start, PIECES[sub])

    def rows_copy(kind, sub):
        quarter = quarters[(1, 0, 0, 1)[kind]]
        rows = rows_of(quarter, sub)
        src = (hidden_in if kind == 0 else hidden_far).at[rows]
        to = (across, beside, left, right)[kind]
        return remote(
            src, hidden_far.at[rows], rows_send.at[kind, sub], rows_recv.at[kind, sub], to
        )

    meta_copy = remote(meta, meta_far, meta_sem.at[0], meta_sem.at[1], across)

    barrier = pltpu.get_barrier_semaphore()
    friends = (up, down, sibling, across, beside, right, left, opposite, farther)
    for friend in friends:
        pl.semaphore_signal(barrier, inc=1, device_id=friend, device_id_type=MESH)
    near_hidden = pltpu.make_async_copy(hidden_in, hidden, near_sem.at[0])
    near_weights = pltpu.make_async_copy(weights_in, place(0, 0, 2), near_sem.at[1])
    near_hidden.start()
    near_weights.start()
    pl.semaphore_wait(barrier, len(friends))

    for hop in (0, 1):
        for way in (0, 1):
            ring_copy(way, hop).start()
    for sub in range(SUBS):
        rows_copy(0, sub).start()
    core_copy(0).start()
    lay_out(ids_in, gates_in, meta)
    meta_copy.start()

    total[...] = jnp.zeros_like(total)
    total_far[...] = jnp.zeros_like(total_far)
    experts = [e for group in range(8) for e in experts_of(group)]

    def ring(step):
        for way in (0, 1):
            ring_copy(way, step).wait_recv()
            if step + 2 < STEPS:
                ring_copy(way, step + 2).start()
        core_copy(step + 1).start()

    def from_across(sub):
        rows_copy(0, sub).wait_recv()
        rows_copy(1, sub).start()
        rows_copy(2, sub).start()

    def from_beside(sub):
        rows_copy(1, sub).wait_recv()
        rows_copy(3, sub).start()

    def pick_near(batch, first, count):
        @pl.loop(first, first + count)
        def _(block):
            pick_rows(
                meta, hidden, picked, block, experts[batch * OWN_BATCH : (batch + 1) * OWN_BATCH]
            )

    def pick_far(turn):
        for kind in (2, 3):
            for sub in range(2 * turn, 2 * turn + 2 + turn // 2):
                rows_copy(kind, sub).wait_recv()

        @pl.loop(0, 4)
        def _(kind):
            odd = x_odd + (kind // 2) * (1 - 2 * x_odd)
            low = y_lo + lax.rem(kind, 2) * (1 - 2 * y_lo)
            block = (odd * 2 + low) * (BLOCKS // 4) + turn
            pick_rows(meta_far, hidden_far, picked_far, block, experts)

    def multiply(acc, rows, column_group, group, half, first=0, count=4):
        left = rows[:, (column_group * 4 + first) * FF : (column_group * 4 + first + count) * FF]
        if half is None:
            start = (group * 4 + first) * FF
            acc[...] += jnp.dot(
                left, held[start : start + count * FF, :], preferred_element_type=jnp.float32
            )
        else:
            start = ((group - WHOLE - 1) * 4 + first) * FF
            acc[:, half * HALF : (half + 1) * HALF] += jnp.dot(
                left, late[half, start : start + count * FF, :], preferred_element_type=jnp.float32
            )

    def multiply_near(group, half=None, first=0, count=4):
        multiply(total, picked, group % 4, group, half, first, count)

    def multiply_far(group, half=None, first=0, count=4):
        multiply(total_far, picked_far, group, group, half, first, count)

    dp_of = lambda x_, y_lo_: y_lo_ * 4 + lax.rem(x_ + 4, 4)
    other = 1 - y_lo
    from_left, from_right, far = dp_of(x - 1, y_lo), dp_of(x + 1, y_lo), dp_of(x + 2, y_lo)
    twin = dp_of(x, other)
    blocks = (
        dp,
        from_left,
        from_right,
        twin,
        far,
        dp_of(x - 1, other),
        dp_of(x + 1, other),
        dp_of(x + 2, other),
    )

    def write(part, number):
        half, first, count = PARTS[part]
        block = blocks[number]
        start = pl.multiple_of(block * COLS + half * HALF, HALF)
        return pltpu.make_async_copy(
            gathered.at[half, block, pl.ds(first, count)],
            out.at[pl.ds(first, count), pl.ds(start, HALF)],
            out_sem.at[part, number],
        )

    def sums_copy(part):
        half, first, count = PARTS[part]
        rows = pl.ds(first, count)
        return remote(
            sent.at[half, rows],
            came.at[half, rows],
            end_send.at[part, 0],
            end_recv.at[part, 0],
            opposite,
        )

    gathers = {
        "mine_up": (1, dp, beside),
        "mine_far": (2, dp, farther),
        "mine_right": (3, dp, right),
        "mine_left": (4, dp, left),
        "twin_right": (5, twin, right),
        "twin_left": (6, twin, left),
        "far_up": (7, far, beside),
    }

    def gather(part, name):
        half, first, count = PARTS[part]
        number, block, to = gathers[name]
        ref = gathered.at[half, block, pl.ds(first, count)]
        return remote(ref, ref, end_send.at[part, number], end_recv.at[part, number], to)

    def send_sums(part):
        half, first, count = PARTS[part]
        rows, columns = slice(first, first + count), slice(half * HALF, (half + 1) * HALF)
        sent[half, rows] = total_far[rows, columns].astype(jnp.bfloat16)
        sums_copy(part).start()

    def finish(part):
        half, first, count = PARTS[part]
        rows, columns = slice(first, first + count), slice(half * HALF, (half + 1) * HALF)
        sums_copy(part).wait_recv()
        gathered[half, dp, rows] = (
            total[rows, columns] + came[half, rows].astype(jnp.float32)
        ).astype(jnp.bfloat16)
        for name in ("mine_up", "mine_far", "mine_right", "mine_left"):
            gather(part, name).start()
        write(part, 0).start()

    def hand_on(part):
        gather(part, "mine_up").wait_recv()
        gather(part, "twin_right").start()
        gather(part, "twin_left").start()
        gather(part, "mine_far").wait_recv()
        gather(part, "far_up").start()
        write(part, 3).start()
        write(part, 4).start()

    def close(part):
        for number, name in (
            (1, "mine_right"),
            (2, "mine_left"),
            (5, "twin_right"),
            (6, "twin_left"),
            (7, "far_up"),
        ):
            gather(part, name).wait_recv()
            write(part, number).start()

    near_hidden.wait()
    pick_near(0, 0, 6)
    from_across(0)
    pick_near(0, 6, 6)
    from_across(1)
    ring(0)
    from_beside(0)
    near_weights.wait()
    core_copy(0).wait_recv()
    multiply_near(0)
    core_copy(1).wait_recv()
    multiply_near(1)
    from_across(2)
    from_beside(1)
    from_across(3)
    ring(1)
    from_beside(2)
    core_copy(2).wait_recv()
    multiply_near(2)
    meta_copy.wait_recv()
    pick_far(0)
    from_across(4)
    from_beside(3)
    ring(2)
    from_across(5)
    from_across(6)
    core_copy(3).wait_recv()
    multiply_near(3)
    from_beside(4)
    pick_near(1, 0, 6)
    from_beside(5)
    from_beside(6)
    pick_far(1)
    ring(3)
    pick_near(1, 6, 6)
    core_copy(4).wait_recv()
    multiply_near(4)
    pick_far(2)
    multiply_far(0)
    ring(4)
    for group in range(1, 5):
        multiply_far(group)
    core_copy(5).wait_recv()
    multiply_near(5)
    multiply_far(5)
    ring(5)
    core_copy(6).wait_recv()
    multiply_near(6, 0)
    multiply_far(6, 0)
    ring(6)
    core_copy(7).wait_recv()
    multiply_far(7, 0)
    send_sums(0)
    multiply_near(7, 0)
    ring(7)
    core_copy(8).wait_recv()
    multiply_near(6, 1)
    multiply_far(6, 1)
    finish(0)
    ring(8)
    multiply_far(7, 1, 0, 2)
    multiply_near(7, 1, 0, 2)
    core_copy(9).wait_recv()
    multiply_far(7, 1, 2, 2)
    send_sums(1)
    send_sums(2)
    multiply_near(7, 1, 2, 2)
    hand_on(0)
    finish(1)
    finish(2)
    hand_on(1)
    hand_on(2)
    for part in range(len(PARTS)):
        close(part)

    for way in (0, 1):
        for step in range(STEPS):
            ring_copy(way, step).wait_send()
    for number in range(STEPS + 1):
        core_copy(number).wait_send()
    for kind in range(4):
        for sub in range(SUBS):
            rows_copy(kind, sub).wait_send()
    meta_copy.wait_send()
    for part in range(len(PARTS)):
        sums_copy(part).wait_send()
        for name in gathers:
            gather(part, name).wait_send()
        for number in range(len(blocks)):
            write(part, number).wait()


def local(hidden, expert_ids, route_gates, down_weight):
    routes = TOKENS * TOP
    anywhere = pl.BlockSpec(memory_space=pl.ANY)
    dma = pltpu.SemaphoreType.DMA
    return pl.pallas_call(
        kernel,
        out_shape=pltpu.VMEM((TOKENS, 8 * COLS), jnp.bfloat16),
        in_specs=[pl.BlockSpec(memory_space=pltpu.VMEM)] * 2 + [anywhere] * 2,
        out_specs=anywhere,
        scratch_shapes=[
            pltpu.VMEM((2 * BLOCKS, ROUTES), jnp.float32),
            pltpu.VMEM((4 * (WHOLE + 1) * FF, COLS), jnp.bfloat16),
            pltpu.VMEM((2, 4 * LATE * FF, HALF), jnp.bfloat16),
            pltpu.VMEM((routes, FF), jnp.bfloat16),
            pltpu.VMEM((routes, FF), jnp.bfloat16),
            pltpu.VMEM((2 * BLOCKS, ROUTES), jnp.float32),
            pltpu.VMEM((TOKENS, OWN_BATCH * FF), jnp.bfloat16),
            pltpu.VMEM((TOKENS, 32 * FF), jnp.bfloat16),
            pltpu.VMEM((TOKENS, COLS), jnp.float32),
            pltpu.VMEM((TOKENS, COLS), jnp.float32),
            pltpu.VMEM((2, TOKENS, HALF), jnp.bfloat16),
            pltpu.VMEM((2, TOKENS, HALF), jnp.bfloat16),
            pltpu.VMEM((2, 8, TOKENS, HALF), jnp.bfloat16),
            dma((2, STEPS)),
            dma((2, STEPS)),
            dma((STEPS + 1,)),
            dma((STEPS + 1,)),
            dma((4, SUBS)),
            dma((4, SUBS)),
            dma((len(PARTS), 8)),
            dma((len(PARTS), 8)),
            dma((2,)),
            dma((2,)),
            dma((len(PARTS), 8)),
        ],
        name="experts",
        compiler_params=pltpu.CompilerParams(
            collective_id=0, has_side_effects=True, vmem_limit_bytes=60 * 2**20
        ),
        cost_estimate=pl.CostEstimate(
            flops=2 * 2 * TOKENS * 32 * FF * COLS * 2,
            bytes_accessed=8 * 2**20,
            transcendentals=0,
        ),
    )(expert_ids.T, route_gates.T, hidden.reshape(routes, FF), down_weight.reshape(2 * FF, COLS))


def solution(mesh):
    placed = (
        P("expert", None, None),
        P("expert", None),
        P("expert", None),
        P("expert", None, "dp"),
    )
    return jax.shard_map(
        local, mesh=mesh, in_specs=placed, out_specs=P("expert", None), check_vma=False
    )
```

time: 104 us -> 96.8 us (0.931); the launches traced: 102 us -> 96.6 us
  local copies, waits for them, and re-layouts: 3.95 us -> 1.15 us
  Pallas kernels: 97 us -> 95.4 us
  other arithmetic: 1.33 us -> 0 us
    unnamed x2 -> x1, local copies, waits for them, and re-layouts: 3.56 us -> 1.15 us
    pallas_call x1, Pallas kernels: 97 us -> 95.4 us  [local(): pl.pallas_call(kernel, out_shape=pltpu.VMEM((TOKENS, 8 * COLS), jnp.bfloa...]
where the time goes in v2:
time: 96.8 us; the launch traced here: 96.6 us
  Pallas kernels  95.4 us (99%)
  local copies, waits for them, and re-layouts  1.15 us (1%)
    pallas_call x1, Pallas kernels, local(): pl.pallas_call(kernel, out_shape=pltpu.VMEM((TOKENS, 8 * COLS), jnp.bfloa...  95.4 us

profile of v2, /device:TPU:16, one launch (start us, length us, event | category | flops | bytes accessed | tf_op | source)
XLA Modules:
  0.0 96.6 jit_solution(2390689489775342381)
XLA Ops:
  0.0 95.4 %experts.1 = bf16[384,2048]{1,0:T(8,128)(2,1)S(1)} custom-call(s32[8,384]{1,0:T(8,128)} %bitcast.6, f32[8,384]{1,0:T(8,128)} %bitcast.7, bf16[3072,768]{1,0:T(8,128)(2,1)} %bitcast.4, bf16[1536,256]{1,0:T(8,128)(2,1)} %bitcast.5), custom_call_target="tpu_custom_call" | custom-call | flops 19327352832 | bytes 8388608 | tf_op jit(solution)/shard_map/experts/pallas_call | solution.py:480
  95.4 1.1 %copy.6 = bf16[384,2048]{1,0:T(8,128)(2,1)} copy(bf16[384,2048]{1,0:T(8,128)(2,1)S(1)} %experts.1) | data formatting | bytes 3145728

commit v3 on v2

--- a/solution.py
+++ b/solution.py
@@ -14,12 +14,12 @@
 COLS = 256
 BLOCK = 32
 BLOCKS = TOKENS // BLOCK
+THREE = 3
 ROUTES = BLOCK * TOP
 HOPS = 7
 QUARTER = TOKENS * TOP // 4
 PIECES = (128, 128, 128, 128, 128, 64, 64)
 SUBS = len(PIECES)
-OWN_BATCH = 16
 WHOLE = 5
 LATE = HOPS - WHOLE
 HALF = COLS // 2
@@ -27,7 +27,7 @@
 PARTS = ((0, 0, TOKENS), (1, 0, TOKENS // 2), (1, TOKENS // 2, TOKENS // 2))
 
 
-def pick_rows(meta, hidden, picked, block, experts):
+def pick_rows(meta, hidden, picked, block, place, experts):
     ids = meta[pl.ds(block, 1), :]
     gates = meta[pl.ds(BLOCKS + block, 1), :]
     shape = (BLOCK, ROUTES)
@@ -44,7 +44,7 @@
     column = jnp.sum(
         jnp.where(diagonal, jnp.broadcast_to(gates, square), 0.0), axis=1, keepdims=True
     )
-    rows = hidden[pl.ds(pl.multiple_of(block * ROUTES, ROUTES), ROUTES), :]
+    rows = hidden[pl.ds(pl.multiple_of(place * ROUTES, ROUTES), ROUTES), :]
     rows = (rows.astype(jnp.float32) * column).astype(jnp.bfloat16)
     result = jnp.dot(chosen, rows, preferred_element_type=jnp.float32).astype(jnp.bfloat16)
     for i in range(len(experts)):
@@ -98,7 +98,6 @@
     total_far,
     sent,
     came,
-    gathered,
     ring_send,
     ring_recv,
     core_send,
@@ -109,7 +108,6 @@
     end_recv,
     meta_sem,
     near_sem,
-    out_sem,
 ):
     dp = lax.axis_index("dp")
     ex = lax.axis_index("expert")
@@ -219,9 +217,17 @@
     friends = (up, down, sibling, across, beside, right, left, opposite, farther)
     for friend in friends:
         pl.semaphore_signal(barrier, inc=1, device_id=friend, device_id_type=MESH)
-    near_hidden = pltpu.make_async_copy(hidden_in, hidden, near_sem.at[0])
-    near_weights = pltpu.make_async_copy(weights_in, place(0, 0, 2), near_sem.at[1])
-    near_hidden.start()
+    def near_hidden(turn):
+        count = THREE * ROUTES
+        return pltpu.make_async_copy(
+            hidden_in.at[pl.ds(turn * count, count)],
+            hidden.at[pl.ds(turn % 2 * count, count)],
+            near_sem.at[1 + turn],
+        )
+
+    near_weights = pltpu.make_async_copy(weights_in, place(0, 0, 2), near_sem.at[0])
+    near_hidden(0).start()
+    near_hidden(1).start()
     near_weights.start()
     pl.semaphore_wait(barrier, len(friends))
 
@@ -254,27 +260,31 @@
         rows_copy(1, sub).wait_recv()
         rows_copy(3, sub).start()
 
-    def pick_near(batch, first, count):
-        @pl.loop(first, first + count)
-        def _(block):
-            pick_rows(
-                meta, hidden, picked, block, experts[batch * OWN_BATCH : (batch + 1) * OWN_BATCH]
-            )
-
-    def pick_far(turn):
-        for kind in (2, 3):
-            for sub in range(2 * turn, 2 * turn + 2 + turn // 2):
-                rows_copy(kind, sub).wait_recv()
-
-        @pl.loop(0, 4)
-        def _(kind):
-            odd = x_odd + (kind // 2) * (1 - 2 * x_odd)
-            low = y_lo + lax.rem(kind, 2) * (1 - 2 * y_lo)
+    def pick_near(turn):
+        near_hidden(turn).wait()
+
+        @pl.loop(0, THREE)
+        def _(i):
+            pick_rows(meta, hidden, picked, turn * THREE + i, turn % 2 * THREE + i, experts)
+
+        if turn + 2 < BLOCKS // THREE:
+            near_hidden(turn + 2).start()
+
+    def pick_far(turn, pair):
+        if pair == 1:
+            for kind in (2, 3):
+                for sub in range(2 * turn, 2 * turn + 2 + turn // 2):
+                    rows_copy(kind, sub).wait_recv()
+        odd = x_odd if pair == 0 else 1 - x_odd
+
+        @pl.loop(0, 2)
+        def _(i):
+            low = y_lo + i * (1 - 2 * y_lo)
             block = (odd * 2 + low) * (BLOCKS // 4) + turn
-            pick_rows(meta_far, hidden_far, picked_far, block, experts)
-
-    def multiply(acc, rows, column_group, group, half, first=0, count=4):
-        left = rows[:, (column_group * 4 + first) * FF : (column_group * 4 + first + count) * FF]
+            pick_rows(meta_far, hidden_far, picked_far, block, block, experts)
+
+    def multiply(acc, rows, group, half, first=0, count=4):
+        left = rows[:, (group * 4 + first) * FF : (group * 4 + first + count) * FF]
         if half is None:
             start = (group * 4 + first) * FF
             acc[...] += jnp.dot(
@@ -287,35 +297,16 @@
             )
 
     def multiply_near(group, half=None, first=0, count=4):
-        multiply(total, picked, group % 4, group, half, first, count)
+        multiply(total, picked, group, half, first, count)
 
     def multiply_far(group, half=None, first=0, count=4):
-        multiply(total_far, picked_far, group, group, half, first, count)
+        multiply(total_far, picked_far, group, half, first, count)
 
     dp_of = lambda x_, y_lo_: y_lo_ * 4 + lax.rem(x_ + 4, 4)
-    other = 1 - y_lo
-    from_left, from_right, far = dp_of(x - 1, y_lo), dp_of(x + 1, y_lo), dp_of(x + 2, y_lo)
-    twin = dp_of(x, other)
-    blocks = (
-        dp,
-        from_left,
-        from_right,
-        twin,
-        far,
-        dp_of(x - 1, other),
-        dp_of(x + 1, other),
-        dp_of(x + 2, other),
-    )
-
-    def write(part, number):
-        half, first, count = PARTS[part]
-        block = blocks[number]
-        start = pl.multiple_of(block * COLS + half * HALF, HALF)
-        return pltpu.make_async_copy(
-            gathered.at[half, block, pl.ds(first, count)],
-            out.at[pl.ds(first, count), pl.ds(start, HALF)],
-            out_sem.at[part, number],
-        )
+    far, twin = dp_of(x + 2, y_lo), dp_of(x, 1 - y_lo)
+
+    def columns_of(block, half):
+        return pl.ds(pl.multiple_of(block * COLS + half * HALF, HALF), HALF)
 
     def sums_copy(part):
         half, first, count = PARTS[part]
@@ -341,7 +332,7 @@
     def gather(part, name):
         half, first, count = PARTS[part]
         number, block, to = gathers[name]
-        ref = gathered.at[half, block, pl.ds(first, count)]
+        ref = out.at[pl.ds(first, count), columns_of(block, half)]
         return remote(ref, ref, end_send.at[part, number], end_recv.at[part, number], to)
 
     def send_sums(part):
@@ -354,12 +345,11 @@
         half, first, count = PARTS[part]
         rows, columns = slice(first, first + count), slice(half * HALF, (half + 1) * HALF)
         sums_copy(part).wait_recv()
-        gathered[half, dp, rows] = (
+        out[rows, columns_of(dp, half)] = (
             total[rows, columns] + came[half, rows].astype(jnp.float32)
         ).astype(jnp.bfloat16)
         for name in ("mine_up", "mine_far", "mine_right", "mine_left"):
             gather(part, name).start()
-        write(part, 0).start()
 
     def hand_on(part):
         gather(part, "mine_up").wait_recv()
@@ -367,66 +357,61 @@
         gather(part, "twin_left").start()
         gather(part, "mine_far").wait_recv()
         gather(part, "far_up").start()
-        write(part, 3).start()
-        write(part, 4).start()
 
     def close(part):
-        for number, name in (
-            (1, "mine_right"),
-            (2, "mine_left"),
-            (5, "twin_right"),
-            (6, "twin_left"),
-            (7, "far_up"),
-        ):
+        for name in ("mine_right", "mine_left", "twin_right", "twin_left", "far_up"):
             gather(part, name).wait_recv()
-            write(part, number).start()
-
-    near_hidden.wait()
-    pick_near(0, 0, 6)
+
+    pick_near(0)
+    pick_near(1)
     from_across(0)
-    pick_near(0, 6, 6)
+    pick_near(2)
     from_across(1)
     ring(0)
     from_beside(0)
+    pick_near(3)
     near_weights.wait()
     core_copy(0).wait_recv()
     multiply_near(0)
-    core_copy(1).wait_recv()
-    multiply_near(1)
     from_across(2)
     from_beside(1)
+    meta_copy.wait_recv()
+    pick_far(0, 0)
     from_across(3)
     ring(1)
     from_beside(2)
-    core_copy(2).wait_recv()
-    multiply_near(2)
-    meta_copy.wait_recv()
-    pick_far(0)
+    core_copy(1).wait_recv()
+    multiply_near(1)
+    pick_far(0, 1)
     from_across(4)
     from_beside(3)
+    pick_far(1, 0)
     ring(2)
     from_across(5)
     from_across(6)
+    from_beside(4)
+    core_copy(2).wait_recv()
+    multiply_near(2)
+    pick_far(1, 1)
+    from_beside(5)
+    from_beside(6)
+    pick_far(2, 0)
     core_copy(3).wait_recv()
     multiply_near(3)
-    from_beside(4)
-    pick_near(1, 0, 6)
-    from_beside(5)
-    from_beside(6)
-    pick_far(1)
     ring(3)
-    pick_near(1, 6, 6)
+    pick_far(2, 1)
+    multiply_far(0)
+    multiply_far(1)
+    ring(4)
+    multiply_far(2)
+    multiply_far(3)
     core_copy(4).wait_recv()
     multiply_near(4)
-    pick_far(2)
-    multiply_far(0)
-    ring(4)
-    for group in range(1, 5):
-        multiply_far(group)
+    multiply_far(4)
+    ring(5)
     core_copy(5).wait_recv()
     multiply_near(5)
     multiply_far(5)
-    ring(5)
     core_copy(6).wait_recv()
     multiply_near(6, 0)
     multiply_far(6, 0)
@@ -447,8 +432,8 @@
     multiply_far(7, 1, 2, 2)
     send_sums(1)
     send_sums(2)
+    hand_on(0)
     multiply_near(7, 1, 2, 2)
-    hand_on(0)
     finish(1)
     finish(2)
     hand_on(1)
@@ -469,8 +454,6 @@
         sums_copy(part).wait_send()
         for name in gathers:
             gather(part, name).wait_send()
-        for number in range(len(blocks)):
-            write(part, number).wait()
 
 
 def local(hidden, expert_ids, route_gates, down_weight):
@@ -481,21 +464,20 @@
         kernel,
         out_shape=pltpu.VMEM((TOKENS, 8 * COLS), jnp.bfloat16),
         in_specs=[pl.BlockSpec(memory_space=pltpu.VMEM)] * 2 + [anywhere] * 2,
-        out_specs=anywhere,
+        out_specs=pl.BlockSpec(memory_space=pltpu.VMEM),
         scratch_shapes=[
             pltpu.VMEM((2 * BLOCKS, ROUTES), jnp.float32),
             pltpu.VMEM((4 * (WHOLE + 1) * FF, COLS), jnp.bfloat16),
             pltpu.VMEM((2, 4 * LATE * FF, HALF), jnp.bfloat16),
-            pltpu.VMEM((routes, FF), jnp.bfloat16),
+            pltpu.VMEM((2 * THREE * ROUTES, FF), jnp.bfloat16),
             pltpu.VMEM((routes, FF), jnp.bfloat16),
             pltpu.VMEM((2 * BLOCKS, ROUTES), jnp.float32),
-            pltpu.VMEM((TOKENS, OWN_BATCH * FF), jnp.bfloat16),
+            pltpu.VMEM((TOKENS, 32 * FF), jnp.bfloat16),
             pltpu.VMEM((TOKENS, 32 * FF), jnp.bfloat16),
             pltpu.VMEM((TOKENS, COLS), jnp.float32),
             pltpu.VMEM((TOKENS, COLS), jnp.float32),
             pltpu.VMEM((2, TOKENS, HALF), jnp.bfloat16),
             pltpu.VMEM((2, TOKENS, HALF), jnp.bfloat16),
-            pltpu.VMEM((2, 8, TOKENS, HALF), jnp.bfloat16),
             dma((2, STEPS)),
             dma((2, STEPS)),
             dma((STEPS + 1,)),
@@ -505,12 +487,11 @@
             dma((len(PARTS), 8)),
             dma((len(PARTS), 8)),
             dma((2,)),
-            dma((2,)),
-            dma((len(PARTS), 8)),
+            dma((1 + BLOCKS // THREE,)),
         ],
         name="experts",
         compiler_params=pltpu.CompilerParams(
-            collective_id=0, has_side_effects=True, vmem_limit_bytes=60 * 2**20
+            collective_id=0, has_side_effects=True, vmem_limit_bytes=61 * 2**20
         ),
         cost_estimate=pl.CostEstimate(
             flops=2 * 2 * TOKENS * 32 * FF * COLS * 2,

time: 96.8 us -> 96.1 us (level)
  no operation moved by 1% of the time
where the time goes in v3:
time: 96.1 us; the launch traced here: 95.9 us
  Pallas kernels  94.8 us (99%)
  local copies, waits for them, and re-layouts  1.15 us (1%)
    pallas_call x1, Pallas kernels, local(): pl.pallas_call(kernel, out_shape=pltpu.VMEM((TOKENS, 8 * COLS), jnp.bfloa...  94.8 us

profile of v3, /device:TPU:16, one launch (start us, length us, event | category | flops | bytes accessed | tf_op | source)
XLA Modules:
  0.0 95.9 jit_solution(10115099268626258078)
XLA Ops:
  0.0 94.8 %experts.1 = bf16[384,2048]{1,0:T(8,128)(2,1)S(1)} custom-call(s32[8,384]{1,0:T(8,128)} %bitcast.6, f32[8,384]{1,0:T(8,128)} %bitcast.7, bf16[3072,768]{1,0:T(8,128)(2,1)} %bitcast.4, bf16[1536,256]{1,0:T(8,128)(2,1)} %bitcast.5), custom_call_target="tpu_custom_call" | custom-call | flops 19327352832 | bytes 8388608 | tf_op jit(solution)/shard_map/experts/pallas_call | solution.py:463
  94.8 1.1 %copy.6 = bf16[384,2048]{1,0:T(8,128)(2,1)} copy(bf16[384,2048]{1,0:T(8,128)(2,1)S(1)} %experts.1) | data formatting | bytes 3145728

commit v4 on v3

--- a/solution.py
+++ b/solution.py
@@ -20,7 +20,7 @@
 QUARTER = TOKENS * TOP // 4
 PIECES = (128, 128, 128, 128, 128, 64, 64)
 SUBS = len(PIECES)
-WHOLE = 5
+WHOLE = 6
 LATE = HOPS - WHOLE
 HALF = COLS // 2
 STEPS = WHOLE + 2 * LATE
@@ -245,10 +245,13 @@
     experts = [e for group in range(8) for e in experts_of(group)]
 
     def ring(step):
+        following = (step + 2,) if step + 2 < WHOLE else ()
+        if step == WHOLE - 2:
+            following = range(WHOLE, STEPS)
         for way in (0, 1):
             ring_copy(way, step).wait_recv()
-            if step + 2 < STEPS:
-                ring_copy(way, step + 2).start()
+            for later in following:
+                ring_copy(way, later).start()
         core_copy(step + 1).start()
 
     def from_across(sub):
@@ -413,29 +416,25 @@
     multiply_near(5)
     multiply_far(5)
     core_copy(6).wait_recv()
-    multiply_near(6, 0)
-    multiply_far(6, 0)
+    multiply_near(6)
+    multiply_far(6)
     ring(6)
     core_copy(7).wait_recv()
     multiply_far(7, 0)
     send_sums(0)
+    ring(7)
     multiply_near(7, 0)
-    ring(7)
-    core_copy(8).wait_recv()
-    multiply_near(6, 1)
-    multiply_far(6, 1)
-    finish(0)
-    ring(8)
     multiply_far(7, 1, 0, 2)
     multiply_near(7, 1, 0, 2)
-    core_copy(9).wait_recv()
+    core_copy(8).wait_recv()
     multiply_far(7, 1, 2, 2)
     send_sums(1)
     send_sums(2)
-    hand_on(0)
+    finish(0)
     multiply_near(7, 1, 2, 2)
     finish(1)
     finish(2)
+    hand_on(0)
     hand_on(1)
     hand_on(2)
     for part in range(len(PARTS)):

time: 96.1 us -> 96.6 us (level); the launches traced: 95.9 us -> 94.8 us
  Pallas kernels: 94.8 us -> 93.6 us
    pallas_call x1, Pallas kernels: 94.8 us -> 93.6 us  [local(): pl.pallas_call(kernel, out_shape=pltpu.VMEM((TOKENS, 8 * COLS), jnp.bfloa...]
where the time goes in v4:
time: 96.6 us; the launch traced here: 94.8 us
  Pallas kernels  93.6 us (97%)
  local copies, waits for them, and re-layouts  1.15 us (1%)
    pallas_call x1, Pallas kernels, local(): pl.pallas_call(kernel, out_shape=pltpu.VMEM((TOKENS, 8 * COLS), jnp.bfloa...  93.6 us

profile of v4, /device:TPU:16, one launch (start us, length us, event | category | flops | bytes accessed | tf_op | source)
XLA Modules:
  0.0 94.8 jit_solution(9380307321501918522)
XLA Ops:
  0.0 93.6 %experts.1 = bf16[384,2048]{1,0:T(8,128)(2,1)S(1)} custom-call(s32[8,384]{1,0:T(8,128)} %bitcast.6, f32[8,384]{1,0:T(8,128)} %bitcast.7, bf16[3072,768]{1,0:T(8,128)(2,1)} %bitcast.4, bf16[1536,256]{1,0:T(8,128)(2,1)} %bitcast.5), custom_call_target="tpu_custom_call" | custom-call | flops 19327352832 | bytes 8388608 | tf_op jit(solution)/shard_map/experts/pallas_call | solution.py:462
  93.6 1.1 %copy.6 = bf16[384,2048]{1,0:T(8,128)(2,1)} copy(bf16[384,2048]{1,0:T(8,128)(2,1)S(1)} %experts.1) | data formatting | bytes 3145728
